TPU v7x, 32 devices: a whole 2x2x4 slice. The times are simulated.
32 devices in a mesh: fab: 4 (over y, x), pts: 8 (over z, core).
Axes of the slice: x: 2, y: 2, z: 4, core: 2. Of those that a mesh axis runs over, the one named last changes fastest.
Arguments:
- fabric_params: float32 [8, 512], P(None, 'fab'), may hold values from -1 to 1
- query_points: float32 [3, 16384], P(None, 'pts'), may hold values from -1 to 1
- cotangent: float32 [3, 512, 16384], P(None, 'fab', 'pts'), may hold values from -0.0078125 to 0.0078125
- branch_first: float32 [8, 256], replicated, may hold values from -2 to 2
- branch_second: float32 [256, 256], replicated, may hold values from -0.375 to 0.375
- branch_out: float32 [256, 768], replicated, may hold values from -0.375 to 0.375
- trunk_first: float32 [3, 256], replicated, may hold values from -3.5 to 3.5
- trunk_second: float32 [256, 256], replicated, may hold values from -0.375 to 0.375
- trunk_out: float32 [256, 256], replicated, may hold values from -0.375 to 0.375
Outputs:
- grad_branch_first: float32 [8, 256], replicated
- grad_branch_second: float32 [256, 256], replicated
- grad_branch_out: float32 [256, 768], replicated
- grad_trunk_first: float32 [3, 256], replicated
- grad_trunk_second: float32 [256, 256], replicated
- grad_trunk_out: float32 [256, 256], replicated
All inputs are finite; a program needn't handle non-finite values.
Results may differ from a plain program's by a relative error of at most 0.000084.
Values sent between devices are 32-bit elements; how exact they have to be, the bound alone decides.
A program may use at most 64 MiB of HBM per device.

v0:
```python
import jax
import jax.numpy as jnp
from jax import lax
from jax.sharding import PartitionSpec as P

HIGH = lax.Precision.HIGHEST


def layers_forward(inputs_t, first, second, out, last_tanh):
    one = jnp.tanh(jnp.einsum("kr,kh->rh", inputs_t, first, precision=HIGH))
    two = jnp.tanh(jnp.dot(one, second, precision=HIGH, preferred_element_type=jnp.float32))
    top = jnp.dot(two, out, precision=HIGH, preferred_element_type=jnp.float32)
    if last_tanh:
        top = jnp.tanh(top)
    return (one, two, top)


def layers_backward(inputs_t, one, two, top_grad, second, out):
    grad_out = jnp.dot(two.T, top_grad, precision=HIGH, preferred_element_type=jnp.float32)
    dtwo = jnp.dot(top_grad, out.T, precision=HIGH, preferred_element_type=jnp.float32) * (
        1.0 - two * two
    )
    grad_second = jnp.dot(one.T, dtwo, precision=HIGH, preferred_element_type=jnp.float32)
    done = jnp.dot(dtwo, second.T, precision=HIGH, preferred_element_type=jnp.float32) * (
        1.0 - one * one
    )
    grad_first = jnp.einsum("kr,rh->kh", inputs_t, done, precision=HIGH)
    return (grad_first, grad_second, grad_out)


def local(
    fabric_params,
    query_points,
    cotangent,
    branch_first,
    branch_second,
    branch_out,
    trunk_first,
    trunk_second,
    trunk_out,
):
    hb1, hb2, coef = layers_forward(fabric_params, branch_first, branch_second, branch_out, False)
    ht1, ht2, basis = layers_forward(query_points, trunk_first, trunk_second, trunk_out, True)
    fab_local = coef.shape[0]
    width = basis.shape[1]
    coef_split = coef.reshape(fab_local, 3, width)
    part_cot = cotangent
    coef_grad = lax.psum(
        jnp.einsum("cfn,np->fcp", part_cot, basis, precision=HIGH).reshape(fab_local, 3 * width),
        "pts",
    )
    local_branch = layers_backward(fabric_params, hb1, hb2, coef_grad, branch_second, branch_out)
    gb1, gb2, gb3 = lax.psum((local_branch[0], local_branch[1], local_branch[2]), "fab")
    part_cot = cotangent
    basis_grad = lax.psum(jnp.einsum("cfn,fcp->np", part_cot, coef_split, precision=HIGH), "fab")
    top_grad = basis_grad * (1.0 - basis * basis)
    local_trunk = layers_backward(query_points, ht1, ht2, top_grad, trunk_second, trunk_out)
    gt1, gt2, gt3 = lax.psum((local_trunk[0], local_trunk[1], local_trunk[2]), "pts")
    return (gb1, gb2, gb3, gt1, gt2, gt3)


def solution(mesh):
    return jax.shard_map(
        local,
        mesh=mesh,
        in_specs=(
            P(None, "fab"),
            P(None, "pts"),
            P(None, "fab", "pts"),
            P(),
            P(),
            P(),
            P(),
            P(),
            P(),
        ),
        out_specs=(P(), P(), P(), P(), P(), P()),
        check_vma=False,
    )
```

profile of v0, /device:TPU:0, one launch (start us, length us, event | category | flops | bytes accessed | tf_op | source)
XLA Modules:
  0.0 233.5 jit_solution(1828818022329271001)
XLA Ops:
  7.2 1.2 convolution_tanh_fusion.4
  8.4 1.2 convolution_tanh_fusion.3
  9.7 2.5 %fusion.7 = f32[128,768]{0,1:T(8,128)S(1)} fusion(f32[128,256]{1,0:T(8,128)S(1)} %convolution_tanh_fusion.3, f32[256,768]{1,0:T(8,128)} %param.14), kind=kOutput, calls=%fused_computation.20 | convolution fusion | flops 301989888 | bytes 1310720 | tf_op jit(solution)/shard_map/dot_general | solution.py:12
  12.2 6.5 %convolution_bitcast_fusion = f32[2048,256]{1,0:T(8,128)} fusion(f32[128,3,256]{0,2,1:T(8,128)S(1)} %bitcast.49, f32[3,128,2048]{2,1,0:T(8,128)S(1)} %copy-done), kind=kOutput, calls=%fused_computation.2 | convolution fusion | flops 2415919104 | bytes 5636096 | tf_op jit(solution)/shard_map/cfn,fcp->np/dot_general | solution.py:55
  19.4 1.9 convolution_tanh_fusion.2
  21.4 1.9 convolution_tanh_fusion.1
  23.3 1.3 copy-done.3
  24.6 1.9 convolution_tanh_fusion
  26.5 1.4 copy-done.5
  27.9 7.9 %fusion = f32[256,3,128]{2,0,1:T(8,128)} fusion(f32[3,128,2048]{2,1,0:T(8,128)S(1)} %copy-done, f32[2048,256]{1,0:T(8,128)S(1)} %convolution_tanh_fusion), kind=kOutput, calls=%fused_computation.6 | convolution fusion | flops 2415919104 | bytes 5636096 | tf_op jit(solution)/shard_map/cfn,np->fcp/dot_general | solution.py:49
  35.8 55.4 %all-reduce.6.cloned.1.call-done = f32[2048,256]{1,0:T(8,128)} async-done(((f32[2048,256]{1,0:T(8,128)}), f32[2048,256]{1,0:T(8,128)}) %all-reduce.6.cloned.1.call-update) | async-done | bytes 2097168 | tf_op jit(solution)/shard_map/psum | solution.py:55
  91.2 5.1 %convolution_multiply_fusion.1 = f32[2048,256]{1,0:T(8,128)S(1)} fusion(f32[256,256]{1,0:T(8,128)} %param.17, f32[2048,256]{1,0:T(8,128)} %copy-done.3, f32[2048,256]{1,0:T(8,128)} %all-reduce.6.cloned.1.call-done, f32[2048,256]{1,0:T(8,128)} %copy-done.5), kind=kOutput, calls=%fused_computation.1 | convolution fusion | flops 1613758464 | bytes 8650752 | tf_op jit(solution)/shard_map/dot_general | solution.py:20
  96.3 4.3 %fusion.8 = f32[256,256]{1,0:T(8,128)} fusion(f32[2048,256]{1,0:T(8,128)S(1)} %copy-done.2, f32[2048,256]{1,0:T(8,128)S(1)} %convolution_multiply_fusion.1), kind=kOutput, calls=%fused_computation.21 | convolution fusion | flops 1610612736 | bytes 4456448 | tf_op jit(solution)/shard_map/dot_general | solution.py:23
  100.6 4.4 %fusion.2 = f32[256,256]{1,0:T(8,128)} fusion(f32[2048,256]{1,0:T(8,128)S(1)} %copy-done.4, f32[2048,256]{1,0:T(8,128)S(1)} %copy-done.8, f32[2048,256]{1,0:T(8,128)S(1)} %copy-done.6), kind=kOutput, calls=%fused_computation.15 | convolution fusion | flops 1612185600 | bytes 6553600 | tf_op jit(solution)/shard_map/dot_general | solution.py:19
  105.4 58.3 %all-reduce.8.cloned.1.call-done = (f32[128,768]{0,1:T(8,128)}, f32[256,256]{1,0:T(8,128)}, f32[256,256]{1,0:T(8,128)}) async-done(((f32[128,768]{0,1:T(8,128)}, f32[256,256]{1,0:T(8,128)}, f32[256,256]{1,0:T(8,128)}), (f32[128,768]{0,1:T(8,128)}, f32[256,256]{1,0:T(8,128)}, f32[256,256]{1,0:T(8,128)})) %all-reduce.8.cloned.1.call-update) | async-done | bytes 917520 | tf_op jit(solution)/shard_map/psum | solution.py:48
  163.7 2.1 convolution_multiply_fusion.3
  165.8 2.7 %fusion.6 = f32[256,768]{1,0:T(8,128)} fusion(f32[128,256]{1,0:T(8,128)S(1)} %convolution_tanh_fusion.3, f32[128,768]{0,1:T(8,128)} %get-tuple-element.6), kind=kOutput, calls=%fused_computation.19 | convolution fusion | flops 301989888 | bytes 1310720 | tf_op jit(solution)/shard_map/dot_general | solution.py:19
  169.6 4.2 %convolution_multiply_fusion = f32[2048,256]{1,0:T(8,128)S(1)} fusion(f32[2048,256]{1,0:T(8,128)} %copy-done.7, f32[256,256]{1,0:T(8,128)} %param.16, f32[2048,256]{1,0:T(8,128)} %copy-done.1), kind=kOutput, calls=%fused_computation | convolution fusion | flops 1612185600 | bytes 6553600 | tf_op jit(solution)/shard_map/dot_general | solution.py:24
  175.0 14.2 %psum.61 = f32[3,256]{1,0:T(4,128)} all-reduce(f32[3,256]{1,0:T(4,128)S(1)} %convolution_bitcast_fusion.2), channel_id=1, replica_groups=mesh['fab'=4,'pts'=8] {'pts'}, use_global_device_ids=true, to_apply=%region_5.0 | all-reduce | flops 768 | bytes 6144 | tf_op jit(solution)/shard_map/psum | solution.py:58
  189.2 1.3 convolution_multiply_fusion.2
  190.8 10.6 %psum.57 = f32[8,256]{1,0:T(8,128)} all-reduce(f32[8,256]{1,0:T(8,128)S(1)} %convolution_bitcast_fusion.1), channel_id=1, replica_groups=mesh['fab'=4,'pts'=8] {'fab'}, use_global_device_ids=true, to_apply=%region_1.0 | all-reduce | flops 2048 | bytes 16384 | tf_op jit(solution)/shard_map/psum | solution.py:53
  201.4 20.4 %all-reduce.10.cloned.1.call-done = (f32[256,256]{1,0:T(8,128)}, f32[256,768]{1,0:T(8,128)}) async-done(((f32[256,256]{1,0:T(8,128)}, f32[256,768]{1,0:T(8,128)}), (f32[256,256]{1,0:T(8,128)}, f32[256,768]{1,0:T(8,128)})) %all-reduce.10.cloned.1.call-update) | async-done | bytes 1048592 | tf_op jit(solution)/shard_map/psum | solution.py:53
  221.8 1.7 copy.32
  223.5 2.1 copy.33
  (43 shorter events, 5.0 us)
Async XLA Ops:
  7.2 5.0 %copy-start = (f32[3,128,2048]{2,1,0:T(8,128)S(1)}, f32[3,128,2048]{2,1,0:T(8,128)}, u32[]{:S(2)}) copy-start(f32[3,128,2048]{2,1,0:T(8,128)} %param.11) | copy-start | bytes 9437188
  7.2 84.0 %all-reduce.6.cloned.1.call-start = ((), (), s32[]{:S(2)}) async-start(), calls=%async_computation | async-start | bytes 4194304 | tf_op jit(solution)/shard_map/psum | solution.py:55
  18.7 0.8 copy-start.13
  18.7 0.8 copy-start.16
  18.7 145.0 %all-reduce.8.cloned.1.call-start = ((), (), s32[]{:S(2)}) async-start(), calls=%async_computation.1 | async-start | bytes 1835008 | tf_op jit(solution)/shard_map/psum | solution.py:48
  19.4 1.9 copy-start.10
  21.4 1.9 copy-start.1
  21.4 3.2 %copy-start.9 = (f32[256,256]{1,0:T(8,128)S(1)}, f32[256,256]{1,0:T(8,128)}, u32[]{:S(2)}) copy-start(f32[256,256]{1,0:T(8,128)} %param.17) | copy-start | bytes 786436
  23.3 1.3 copy-start.3
  26.5 1.4 copy-start.5
  91.2 5.1 %copy-start.2 = (f32[2048,256]{1,0:T(8,128)S(1)}, f32[2048,256]{1,0:T(8,128)}, u32[]{:S(2)}) copy-start(f32[2048,256]{1,0:T(8,128)} %copy-done.1) | copy-start | bytes 6291460
  91.2 9.4 %copy-start.8 = (f32[2048,256]{1,0:T(8,128)S(1)}, f32[2048,256]{1,0:T(8,128)}, u32[]{:S(2)}) copy-start(f32[2048,256]{1,0:T(8,128)} %all-reduce.6.cloned.1.call-done) | copy-start | bytes 6291460
  96.3 4.3 %copy-start.7 = (f32[2048,256]{1,0:T(8,128)}, f32[2048,256]{1,0:T(8,128)S(1)}, u32[]{:S(2)}) copy-start(f32[2048,256]{1,0:T(8,128)S(1)} %convolution_multiply_fusion.1) | copy-start | bytes 6291460
  96.3 4.3 %copy-start.4 = (f32[2048,256]{1,0:T(8,128)S(1)}, f32[2048,256]{1,0:T(8,128)}, u32[]{:S(2)}) copy-start(f32[2048,256]{1,0:T(8,128)} %copy-done.3) | copy-start | bytes 6291460
  96.3 4.3 %copy-start.6 = (f32[2048,256]{1,0:T(8,128)S(1)}, f32[2048,256]{1,0:T(8,128)}, u32[]{:S(2)}) copy-start(f32[2048,256]{1,0:T(8,128)} %copy-done.5) | copy-start | bytes 6291460
  105.1 116.7 %all-reduce.10.cloned.1.call-start = ((), (), s32[]{:S(2)}) async-start(), calls=%async_computation.2 | async-start | bytes 2097152 | tf_op jit(solution)/shard_map/psum | solution.py:53
  169.6 4.3 %copy-start.14 = (f32[3,2048]{1,0:T(4,128)S(1)}, f32[3,2048]{1,0:T(4,128)}, u32[]{:S(2)}) copy-start(f32[3,2048]{1,0:T(4,128)} %param.10) | copy-start | bytes 73732
  173.9 16.7 %copy-start.15 = (f32[8,128]{1,0:T(8,128)S(1)}, f32[8,128]{1,0:T(8,128)}, u32[]{:S(2)}) copy-start(f32[8,128]{1,0:T(8,128)} %param.9) | copy-start | bytes 12292
  190.8 35.5 %copy-start.11 = (f32[256,256]{1,0:T(8,128)S(1)}, f32[256,256]{1,0:T(8,128)}, u32[]{:S(2)}) copy-start(f32[256,256]{1,0:T(8,128)} %get-tuple-element.16) | copy-start | bytes 786436
  221.7 3.8 %copy-start.12 = (f32[256,256]{1,0:T(8,128)S(1)}, f32[256,256]{1,0:T(8,128)}, u32[]{:S(2)}) copy-start(f32[256,256]{1,0:T(8,128)} %get-tuple-element.15) | copy-start | bytes 786436
Sparse Core Ops, SparseCore 0:
  18.8 72.3 all-reduce.5
  105.2 58.4 all-reduce.7
  169.7 51.9 all-reduce.9
where the time goes:
time: 234 us; the launch traced here: 233 us
  waiting for transfers between devices  134 us (57%)
  matrix products  51.5 us (22%)
  blocking collectives  24.8 us (11%)
  between operations  14 us (6%)
  local copies, waits for them, and re-layouts  8.44 us (4%)
    psum x1, waiting for transfers between devices, local(): lax.psum(jnp.einsum('cfn,np->fcp', part_cot, basis, precision=HIGH).resha...  58.3 us
    psum x1, waiting for transfers between devices, local(): lax.psum(jnp.einsum('cfn,fcp->np', part_cot, coef_split, precision=HIGH),...  55.4 us
    psum x1, waiting for transfers between devices, local(): lax.psum((local_branch[0], local_branch[1], local_branch[2]), 'fab')  20.4 us
    psum x1, blocking collectives, local(): lax.psum((local_trunk[0], local_trunk[1], local_trunk[2]), 'pts')  14.2 us
    psum x1, blocking collectives, local(): lax.psum((local_branch[0], local_branch[1], local_branch[2]), 'fab')  10.6 us
    unnamed x38, local copies, waits for them, and re-layouts  8.44 us
    dot_general x1, matrix products, local(): jnp.einsum('cfn,np->fcp', part_cot, basis, precision=HIGH)  7.94 us
    dot_general x2, matrix products, layers_backward(): jnp.dot(top_grad, out.T, precision=HIGH, preferred_element_type=jnp.float32)  7.11 us
  transfers between devices with their start and end apart: 3, of which 3 were waited for; matrix products, arithmetic and copies ran while one was open for 9% of the time, Pallas kernels for 0%

commit v1 on v0

--- a/solution.py
+++ b/solution.py
@@ -3,7 +3,7 @@
 from jax import lax
 from jax.sharding import PartitionSpec as P
 
-HIGH = lax.Precision.HIGHEST
+HIGH = lax.Precision.HIGH
 
 
 def layers_forward(inputs_t, first, second, out, last_tanh):
@@ -44,18 +44,12 @@
     fab_local = coef.shape[0]
     width = basis.shape[1]
     coef_split = coef.reshape(fab_local, 3, width)
-    part_cot = cotangent
-    coef_grad = lax.psum(
-        jnp.einsum("cfn,np->fcp", part_cot, basis, precision=HIGH).reshape(fab_local, 3 * width),
-        "pts",
-    )
-    local_branch = layers_backward(fabric_params, hb1, hb2, coef_grad, branch_second, branch_out)
-    gb1, gb2, gb3 = lax.psum((local_branch[0], local_branch[1], local_branch[2]), "fab")
-    part_cot = cotangent
-    basis_grad = lax.psum(jnp.einsum("cfn,fcp->np", part_cot, coef_split, precision=HIGH), "fab")
+    basis_grad = jnp.einsum("cfn,fcp->np", cotangent, coef_split, precision=HIGH)
     top_grad = basis_grad * (1.0 - basis * basis)
     local_trunk = layers_backward(query_points, ht1, ht2, top_grad, trunk_second, trunk_out)
-    gt1, gt2, gt3 = lax.psum((local_trunk[0], local_trunk[1], local_trunk[2]), "pts")
+    coef_grad = jnp.einsum("cfn,np->fcp", cotangent, basis, precision=HIGH).reshape(fab_local, 3 * width)
+    local_branch = layers_backward(fabric_params, hb1, hb2, coef_grad, branch_second, branch_out)
+    gb1, gb2, gb3, gt1, gt2, gt3 = lax.psum(local_branch + local_trunk, ("fab", "pts"))
     return (gb1, gb2, gb3, gt1, gt2, gt3)
 
 

time: 234 us -> 180 us (0.77)
  waiting for transfers between devices: 134 us -> 88.5 us
  matrix products: 51.5 us -> 29.5 us
  blocking collectives: 24.8 us -> 42.1 us
  local copies, waits for them, and re-layouts: 8.44 us -> 5.47 us
    psum x3 -> x1, waiting for transfers between devices: 134 us -> 88.5 us  [local(): lax.psum(local_branch + local_trunk, ('fab', 'pts'))]
    psum x2 -> x1, blocking collectives: 24.8 us -> 42.1 us  [local(): lax.psum(local_branch + local_trunk, ('fab', 'pts'))]
    dot_general x2, matrix products: 14.4 us -> 6.31 us  [the longest x1 3.52 us: local(): jnp.einsum('cfn,np->fcp', cotangent, basis, precision=HIGH)]
    dot_general x2, matrix products: 7.11 us -> 1.61 us  [layers_backward(): jnp.dot(top_grad, out.T, precision=HIGH, preferred_element_type=jnp.float32)]
    unnamed x38 -> x24, local copies, waits for them, and re-layouts: 8.44 us -> 5.47 us
    dot_general x2, matrix products: 7.09 us -> 4.17 us  [layers_backward(): jnp.dot(two.T, top_grad, precision=HIGH, preferred_element_type=jnp.float32)]
  transfers between devices with their start and end apart: 3 -> 1, of which waited for: 3 -> 1; matrix products, arithmetic and copies ran while one was open for 9% -> 3% of each run, Pallas kernels for 0% -> 0%
where the time goes in v1:
time: 180 us
  waiting for transfers between devices  88.5 us (49%)
  blocking collectives  42.1 us (23%)
  matrix products  29.5 us (16%)
  between operations  14.2 us (8%)
  local copies, waits for them, and re-layouts  5.47 us (3%)
    psum x1, waiting for transfers between devices, local(): lax.psum(local_branch + local_trunk, ('fab', 'pts'))  88.5 us
    psum x1, blocking collectives, local(): lax.psum(local_branch + local_trunk, ('fab', 'pts'))  42.1 us
    unnamed x24, local copies, waits for them, and re-layouts  5.47 us
    dot_general x2, matrix products, layers_backward(): jnp.dot(dtwo, second.T, precision=HIGH, preferred_element_type=jnp.float32)  4.64 us
    dot_general x2, matrix products, layers_backward(): jnp.dot(two.T, top_grad, precision=HIGH, preferred_element_type=jnp.float32)  4.17 us
    dot_general x2, matrix products, layers_backward(): jnp.dot(one.T, dtwo, precision=HIGH, preferred_element_type=jnp.float32)  3.92 us
  transfers between devices with their start and end apart: 1, of which 1 were waited for; matrix products, arithmetic and copies ran while one was open for 3% of the time, Pallas kernels for 0%

profile of v1, /device:TPU:0, one launch (start us, length us, event | category | flops | bytes accessed | tf_op | source)
XLA Modules:
  0.0 179.8 jit_solution(2051328933813977361)
XLA Ops:
  7.2 1.1 convolution_tanh_fusion.4
  8.4 1.2 convolution_tanh_fusion.3
  9.6 1.9 %fusion.5 = f32[128,768]{0,1:T(8,128)S(1)} fusion(f32[128,256]{1,0:T(8,128)S(1)} %convolution_tanh_fusion.3, f32[256,768]{1,0:T(8,128)} %param.14), kind=kOutput, calls=%fused_computation.17 | convolution fusion | flops 150994944 | bytes 1310720 | tf_op jit(solution)/shard_map/dot_general | solution.py:12
  11.5 1.8 %convolution_tanh_fusion.2 = f32[2048,256]{1,0:T(8,128)S(1)} fusion(f32[3,2048]{1,0:T(4,128)} %param.10, f32[3,256]{1,0:T(4,128)} %param.15), kind=kOutput, calls=%fused_computation.6 | convolution fusion | flops 9437184 | bytes 2124800 | tf_op jit(solution)/shard_map/kr,kh->rh/dot_general | solution.py:10
  13.4 1.0 convolution_tanh_fusion.1
  14.5 1.0 convolution_tanh_fusion
  15.5 3.5 %fusion.1 = f32[256,3,128]{2,0,1:T(8,128)S(1)} fusion(f32[3,128,2048]{2,1,0:T(8,128)S(1)} %copy-done, f32[2048,256]{1,0:T(8,128)S(1)} %convolution_tanh_fusion), kind=kOutput, calls=%fused_computation.7 | convolution fusion | flops 1207959552 | bytes 5636096 | tf_op jit(solution)/shard_map/cfn,np->fcp/dot_general | solution.py:50
  19.1 0.6 convolution_multiply_fusion.3
  19.6 1.4 fusion.4
  21.0 2.8 %fusion = f32[2048,256]{1,0:T(8,128)S(1)} fusion(f32[128,3,256]{0,2,1:T(8,128)S(1)} %bitcast.54, f32[3,128,2048]{2,1,0:T(8,128)S(1)} %copy-done, f32[2048,256]{1,0:T(8,128)S(1)} %convolution_tanh_fusion), kind=kOutput, calls=%fused_computation.3 | convolution fusion | flops 1209532416 | bytes 7733248 | tf_op jit(solution)/shard_map/cfn,fcp->np/dot_general | solution.py:47
  23.8 2.8 %fusion.7 = f32[256,256]{1,0:T(8,128)} fusion(f32[2048,256]{1,0:T(8,128)S(1)} %convolution_tanh_fusion.1, f32[2048,256]{1,0:T(8,128)S(1)} %fusion), kind=kOutput, calls=%fused_computation.19 | convolution fusion | flops 805306368 | bytes 4456448 | tf_op jit(solution)/shard_map/dot_general | solution.py:19
  26.6 1.1 convolution_multiply_fusion.1
  27.7 1.3 fusion.3
  29.1 2.6 %fusion.6 = f32[256,256]{1,0:T(8,128)} fusion(f32[2048,256]{1,0:T(8,128)S(1)} %convolution_tanh_fusion.2, f32[2048,256]{1,0:T(8,128)S(1)} %convolution_multiply_fusion.1), kind=kOutput, calls=%fused_computation.18 | convolution fusion | flops 805306368 | bytes 4456448 | tf_op jit(solution)/shard_map/dot_general | solution.py:23
  31.7 1.3 convolution_multiply_fusion.2
  33.0 0.1 convolution_bitcast_fusion.1
  33.2 3.4 %convolution_multiply_fusion = f32[2048,256]{1,0:T(8,128)S(1)} fusion(f32[2048,256]{1,0:T(8,128)} %copy-done.2, f32[256,256]{1,0:T(8,128)} %param.16, f32[2048,256]{1,0:T(8,128)} %copy-done.1), kind=kOutput, calls=%fused_computation | convolution fusion | flops 806879232 | bytes 6553600 | tf_op jit(solution)/shard_map/dot_general | solution.py:24
  36.6 0.6 convolution_bitcast_fusion.2
  37.2 42.1 %all-reduce = (f32[8,256]{1,0:T(8,128)}, f32[3,256]{1,0:T(4,128)}) all-reduce(f32[8,256]{1,0:T(8,128)S(1)} %convolution_bitcast_fusion.1, f32[3,256]{1,0:T(4,128)S(1)} %convolution_bitcast_fusion.2), channel_id=1, replica_groups=mesh['fab'=4,'pts'=8] {'fab','pts'}, use_global_device_ids=true, to_apply=%region_0.0 | all-reduce | flops 2816 | bytes 22528 | tf_op jit(solution)/shard_map/psum | solution.py:52
  79.3 88.5 %all-reduce.4.cloned.1.call-done = (f32[256,256]{1,0:T(8,128)}, f32[256,768]{1,0:T(8,128)}, f32[256,256]{1,0:T(8,128)}, f32[256,256]{1,0:T(8,128)}) async-done(((f32[256,256]{1,0:T(8,128)}, f32[256,768]{1,0:T(8,128)}, f32[256,256]{1,0:T(8,128)}, f32[256,256]{1,0:T(8,128)}), (f32[256,256]{1,0:T(8,128)}, f32[256,768]{1,0:T(8,128)}, f32[256,256]{1,0:T(8,128)}, ...) | async-done | bytes 1572880 | tf_op jit(solution)/shard_map/psum | solution.py:52
  167.8 1.7 copy.30
  169.5 2.1 %copy.31 = f32[256,768]{1,0:T(8,128)} copy(f32[256,768]{1,0:T(8,128)} %get-tuple-element.14) | data formatting | bytes 1572864
  171.6 0.7 copy.32
  172.3 0.7 copy.33
  (22 shorter events, 0.3 us)
Async XLA Ops:
  7.2 8.4 %copy-start = (f32[3,128,2048]{2,1,0:T(8,128)S(1)}, f32[3,128,2048]{2,1,0:T(8,128)}, u32[]{:S(2)}) copy-start(f32[3,128,2048]{2,1,0:T(8,128)} %param.11) | copy-start | bytes 9437188
  7.2 6.2 %copy-start.5 = (f32[256,256]{1,0:T(8,128)S(1)}, f32[256,256]{1,0:T(8,128)}, u32[]{:S(2)}) copy-start(f32[256,256]{1,0:T(8,128)} %param.16) | copy-start | bytes 786436
  7.2 160.6 %all-reduce.4.cloned.1.call-start = ((), (), s32[]{:S(2)}) async-start(), calls=%async_computation | async-start | bytes 3145728 | tf_op jit(solution)/shard_map/psum | solution.py:52
  13.4 15.6 %copy-start.1 = (f32[2048,256]{1,0:T(8,128)}, f32[2048,256]{1,0:T(8,128)S(1)}, u32[]{:S(2)}) copy-start(f32[2048,256]{1,0:T(8,128)S(1)} %convolution_tanh_fusion.2) | copy-start | bytes 6291460
  13.4 1.1 copy-start.4
  15.5 3.5 %copy-start.3 = (f32[256,768]{1,0:T(8,128)S(1)}, f32[256,768]{1,0:T(8,128)}, u32[]{:S(2)}) copy-start(f32[256,768]{1,0:T(8,128)} %param.14) | copy-start | bytes 2359300
  27.7 1.4 copy-start.2
  31.7 1.3 copy-start.9
  33.2 3.4 %copy-start.8 = (f32[3,2048]{1,0:T(4,128)S(1)}, f32[3,2048]{1,0:T(4,128)}, u32[]{:S(2)}) copy-start(f32[3,2048]{1,0:T(4,128)} %param.10) | copy-start | bytes 73732
  167.8 3.8 %copy-start.7 = (f32[256,256]{1,0:T(8,128)S(1)}, f32[256,256]{1,0:T(8,128)}, u32[]{:S(2)}) copy-start(f32[256,256]{1,0:T(8,128)} %get-tuple-element.16) | copy-start | bytes 786436
  167.8 4.5 %copy-start.6 = (f32[256,256]{1,0:T(8,128)S(1)}, f32[256,256]{1,0:T(8,128)}, u32[]{:S(2)}) copy-start(f32[256,256]{1,0:T(8,128)} %get-tuple-element.17) | copy-start | bytes 786436
Sparse Core Ops, SparseCore 0:
  31.9 135.8 all-reduce.3

commit v2 on v1

--- a/solution.py
+++ b/solution.py
@@ -1,9 +1,15 @@
+import functools
+
 import jax
 import jax.numpy as jnp
 from jax import lax
+from jax.experimental import pallas as pl
+from jax.experimental.pallas import tpu as pltpu
 from jax.sharding import PartitionSpec as P
 
 HIGH = lax.Precision.HIGH
+MESH = pl.DeviceIdType.MESH
+LANES = 128
 
 
 def layers_forward(inputs_t, first, second, out, last_tanh):
@@ -28,7 +34,199 @@
     return (grad_first, grad_second, grad_out)
 
 
+class Plan:
+    def __init__(self, rows, nf, nq):
+        self.nf, self.nq = nf, nq
+        unit = 8 * nf * nq
+        units = -(-rows // (2 * unit))
+        a = max(1, (9 * units + 6) // 13)
+        self.ra, self.rb = a * unit, (units - a) * unit
+        self.half = self.ra + self.rb
+        self.total = 2 * self.half
+        self.pa, self.pb = self.ra // nf, self.rb // nq
+        self.sa, self.sb = self.pa // nq, self.pb // nf
+        self.count = 1 + 2 * 2 * (nf - 1 + nq - 1) + nf + nq
+
+    def scratch(self):
+        f32 = jnp.float32
+        return [
+            pltpu.VMEM((self.total, LANES), f32),
+            pltpu.VMEM((self.total, LANES), f32),
+            pltpu.VMEM((self.half, LANES), f32),
+            pltpu.VMEM((max(self.nf - 1, 1), self.pa, LANES), f32),
+            pltpu.VMEM((max(self.nq - 1, 1), max(self.pb, 8), LANES), f32),
+            pltpu.VMEM((max(self.nq - 1, 1), self.sa, LANES), f32),
+            pltpu.VMEM((max(self.nf - 1, 1), max(self.sb, 8), LANES), f32),
+            pltpu.SemaphoreType.DMA((self.count,)),
+            pltpu.SemaphoreType.DMA((self.count,)),
+        ]
+
+
+def where(plan):
+    f = lax.axis_index("fab")
+    p = lax.axis_index("pts")
+    return f, p // 2, p % 2
+
+
+def greet(plan):
+    f, q, c = where(plan)
+    barrier = pltpu.get_barrier_semaphore()
+    peers = [(f, 2 * q + 1 - c)]
+    peers += [(lax.rem(f + k, plan.nf), 2 * q + c) for k in range(1, plan.nf)]
+    peers += [(f, 2 * lax.rem(q + k, plan.nq) + c) for k in range(1, plan.nq)]
+    for peer in peers:
+        pl.semaphore_signal(barrier, inc=1, device_id=peer, device_id_type=MESH)
+    pl.semaphore_wait(barrier, len(peers))
+
+
+def sum_over_all(plan, acc, res, core_in, a1, b1, a2, b2, send, recv):
+    nf, nq = plan.nf, plan.nq
+    ra, pa, sa, pb, sb = plan.ra, plan.pa, plan.sa, plan.pb, plan.sb
+    f, q, c = where(plan)
+    has_b = plan.rb > 0
+    used, started = [0], []
+
+    def rows(start, size):
+        return pl.ds(pl.multiple_of(start, 8), size)
+
+    def go(src, dst, peer):
+        index = used[0]
+        used[0] += 1
+        copy = pltpu.make_async_remote_copy(
+            src_ref=src,
+            dst_ref=dst,
+            send_sem=send.at[index],
+            recv_sem=recv.at[index],
+            device_id=peer,
+            device_id_type=MESH,
+        )
+        copy.start()
+        started.append(copy)
+        return copy
+
+    def fab_peers():
+        return [(k, lax.rem(f + k, nf)) for k in range(1, nf)]
+
+    def pts_peers():
+        return [(k, lax.rem(q + k, nq)) for k in range(1, nq)]
+
+    def at_fab(d):
+        return (d, 2 * q + c)
+
+    def at_pts(d):
+        return (f, 2 * d + c)
+
+    sibling = (f, 2 * q + 1 - c)
+    mine = c * plan.half
+    other = (1 - c) * plan.half
+
+    go(acc.at[rows(other, plan.half)], core_in, sibling).wait_recv()
+    acc[rows(mine, plan.half), :] += core_in[...]
+
+    base_a = mine + f * pa
+    base_b = mine + ra + q * pb
+    own_a = base_a + q * sa
+    own_b = base_b + f * sb
+
+    first_a = [go(acc.at[rows(mine + d * pa, pa)], a1.at[k - 1], at_fab(d)) for k, d in fab_peers()]
+    first_b = []
+    if has_b:
+        first_b = [
+            go(acc.at[rows(mine + ra + d * pb, pb)], b1.at[k - 1], at_pts(d)) for k, d in pts_peers()
+        ]
+
+    def add_up(into, start, size, slots, copies):
+        value = acc[rows(start, size), :]
+        for k, copy in enumerate(copies):
+            copy.wait_recv()
+            value = value + slots[k]
+        into[rows(start, size), :] = value
+
+    add_up(acc, base_a, pa, a1, first_a)
+    second_a = [go(acc.at[rows(base_a + d * sa, sa)], a2.at[k - 1], at_pts(d)) for k, d in pts_peers()]
+    second_b = []
+    if has_b:
+        add_up(acc, base_b, pb, b1, first_b)
+        second_b = [
+            go(acc.at[rows(base_b + d * sb, sb)], b2.at[k - 1], at_fab(d)) for k, d in fab_peers()
+        ]
+
+    def give(start, size, peer):
+        part = res.at[rows(start, size)]
+        return go(part, part, peer)
+
+    add_up(res, own_a, sa, a2, second_a)
+    third_a = [give(own_a, sa, at_pts(d)) for _, d in pts_peers()]
+    third_b = []
+    if has_b:
+        add_up(res, own_b, sb, b2, second_b)
+        third_b = [give(own_b, sb, at_fab(d)) for _, d in fab_peers()]
+
+    last = []
+    for copy in third_a:
+        copy.wait_recv()
+    fourth_a = [give(base_a, pa, at_fab(d)) for _, d in fab_peers()]
+    last.append(give(base_a, pa, sibling))
+    fourth_b = []
+    if has_b:
+        for copy in third_b:
+            copy.wait_recv()
+        fourth_b = [give(base_b, pb, at_pts(d)) for _, d in pts_peers()]
+        last.append(give(base_b, pb, sibling))
+    for k, copy in enumerate(fourth_a):
+        copy.wait_recv()
+        last.append(give(mine + lax.rem(f + nf - 1 - k, nf) * pa, pa, sibling))
+    for k, copy in enumerate(fourth_b):
+        copy.wait_recv()
+        last.append(give(mine + ra + lax.rem(q + nq - 1 - k, nq) * pb, pb, sibling))
+    for copy in last:
+        copy.wait_recv()
+    for copy in started:
+        copy.wait_send()
+
+
+def pieces(shapes):
+    table, start = [], 0
+    for i, (r, w) in enumerate(shapes):
+        kept = -(-r // 8) * 8
+        for col in range(0, w, LANES):
+            table.append((i, col, r, kept, start))
+            start += kept
+    return table, start
+
+
+def sum_kernel(plan, table, n, *refs):
+    ins, outs = refs[:n], refs[n : 2 * n]
+    acc, res, *rest = refs[2 * n :]
+    greet(plan)
+    acc[...] = jnp.zeros_like(acc)
+    for i, col, r, _, start in table:
+        acc[start : start + r, :] = ins[i][:, col : col + LANES]
+    sum_over_all(plan, acc, res, *rest)
+    for i, col, r, _, start in table:
+        outs[i][:, col : col + LANES] = res[start : start + r, :]
+
+
+def summed(grads, nf, nq):
+    shapes = [g.shape for g in grads]
+    table, rows = pieces(shapes)
+    plan = Plan(rows, nf, nq)
+    vmem = pl.BlockSpec(memory_space=pltpu.VMEM)
+    return pl.pallas_call(
+        functools.partial(sum_kernel, plan, table, len(grads)),
+        out_shape=[jax.ShapeDtypeStruct(s, jnp.float32) for s in shapes],
+        in_specs=[vmem] * len(grads),
+        out_specs=[vmem] * len(grads),
+        scratch_shapes=plan.scratch(),
+        compiler_params=pltpu.CompilerParams(
+            collective_id=0, has_side_effects=True, vmem_limit_bytes=40 * 1024 * 1024
+        ),
+    )(*grads)
+
+
 def local(
+    nf,
+    nq,
     fabric_params,
     query_points,
     cotangent,
@@ -47,15 +245,18 @@
     basis_grad = jnp.einsum("cfn,fcp->np", cotangent, coef_split, precision=HIGH)
     top_grad = basis_grad * (1.0 - basis * basis)
     local_trunk = layers_backward(query_points, ht1, ht2, top_grad, trunk_second, trunk_out)
-    coef_grad = jnp.einsum("cfn,np->fcp", cotangent, basis, precision=HIGH).reshape(fab_local, 3 * width)
+    coef_grad = jnp.einsum("cfn,np->fcp", cotangent, basis, precision=HIGH).reshape(
+        fab_local, 3 * width
+    )
     local_branch = layers_backward(fabric_params, hb1, hb2, coef_grad, branch_second, branch_out)
-    gb1, gb2, gb3, gt1, gt2, gt3 = lax.psum(local_branch + local_trunk, ("fab", "pts"))
-    return (gb1, gb2, gb3, gt1, gt2, gt3)
+    return tuple(summed(local_branch + local_trunk, nf, nq))
 
 
 def solution(mesh):
+    nf = mesh.shape["fab"]
+    nq = mesh.shape["pts"] // 2
     return jax.shard_map(
-        local,
+        functools.partial(local, nf, nq),
         mesh=mesh,
         in_specs=(
             P(None, "fab"),

time: 180 us -> 62.4 us (0.35)
  waiting for transfers between devices: 88.5 us -> 0 us
  blocking collectives: 42.1 us -> 0 us
  Pallas kernels: 0 us -> 34.2 us
  between operations: 14.2 us -> 0.88 us
  matrix products: 29.5 us -> 22.9 us
    psum x1 -> x0, waiting for transfers between devices: 88.5 us -> none  [local(): lax.psum(local_branch + local_trunk, ('fab', 'pts'))]
    psum x1 -> x0, blocking collectives: 42.1 us -> none  [local(): lax.psum(local_branch + local_trunk, ('fab', 'pts'))]
    pallas_call x0 -> x1, Pallas kernels: none -> 34.2 us  [summed(): pl.pallas_call(functools.partial(sum_kernel, plan, table, len(grads)), ou...]
    dot_general x2, matrix products: 4.64 us -> 1.36 us  [layers_backward(): jnp.dot(dtwo, second.T, precision=HIGH, preferred_element_type=jnp.float32)]
    unnamed x24 -> x20, local copies, waits for them, and re-layouts: 5.47 us -> 4.22 us
  transfers between devices with their start and end apart: 1 -> 0, of which waited for: 1 -> 0; matrix products, arithmetic and copies ran while one was open for 3% -> 0% of each run, Pallas kernels for 0% -> 0%
where the time goes in v2:
time: 62.4 us; the launch traced here: 62.2 us
  Pallas kernels  34.2 us (55%)
  matrix products  22.9 us (37%)
  local copies, waits for them, and re-layouts  4.22 us (7%)
  between operations  0.88 us (1%)
    pallas_call x1, Pallas kernels, summed(): pl.pallas_call(functools.partial(sum_kernel, plan, table, len(grads)), ou...  34.2 us
    unnamed x20, local copies, waits for them, and re-layouts  4.22 us
    dot_general x1, matrix products, local(): jnp.einsum('cfn,np->fcp', cotangent, basis, precision=HIGH)  3.52 us
    dot_general x2, matrix products, layers_forward(): one = jnp.tanh(jnp.einsum('kr,kh->rh', inputs_t, first, precision=HIGH))  2.94 us
    dot_general x2, matrix products, layers_forward(): top = jnp.dot(two, out, precision=HIGH, preferred_element_type=jnp.float32)  2.93 us
    dot_general x1, matrix products, local(): jnp.einsum('cfn,fcp->np', cotangent, coef_split, precision=HIGH)  2.79 us
    dot_general x2, matrix products, layers_backward(): jnp.dot(two.T, top_grad, precision=HIGH, preferred_element_type=jnp.float32)  2.57 us
    dot_general x2, matrix products, layers_backward(): jnp.dot(one.T, dtwo, precision=HIGH, preferred_element_type=jnp.float32)  2.26 us

profile of v2, /device:TPU:0, one launch (start us, length us, event | category | flops | bytes accessed | tf_op | source)
XLA Modules:
  0.0 62.2 jit_solution(11573265105156502864)
XLA Ops:
  0.7 1.1 %convolution_tanh_fusion.4 = f32[128,256]{1,0:T(8,128)S(1)} fusion(f32[8,128]{1,0:T(8,128)} %param.9, f32[8,256]{1,0:T(8,128)} %param.12), kind=kOutput, calls=%fused_computation.12 | convolution fusion | flops 1572864 | bytes 143360 | tf_op jit(solution)/shard_map/kr,kh->rh/dot_general | solution.py:16
  1.8 1.2 %convolution_tanh_fusion.3 = f32[128,256]{1,0:T(8,128)S(1)} fusion(f32[128,256]{1,0:T(8,128)S(1)} %convolution_tanh_fusion.4, f32[256,256]{1,0:T(8,128)} %param.13), kind=kOutput, calls=%fused_computation.10 | convolution fusion | flops 50331648 | bytes 524288 | tf_op jit(solution)/shard_map/dot_general | solution.py:17
  3.0 1.9 %fusion.5 = f32[128,768]{0,1:T(8,128)S(1)} fusion(f32[128,256]{1,0:T(8,128)S(1)} %convolution_tanh_fusion.3, f32[256,768]{1,0:T(8,128)} %param.14), kind=kOutput, calls=%fused_computation.17 | convolution fusion | flops 150994944 | bytes 1310720 | tf_op jit(solution)/shard_map/dot_general | solution.py:18
  4.9 1.8 %convolution_tanh_fusion.2 = f32[2048,256]{1,0:T(8,128)S(1)} fusion(f32[3,2048]{1,0:T(4,128)} %param.10, f32[3,256]{1,0:T(4,128)} %param.15), kind=kOutput, calls=%fused_computation.6 | convolution fusion | flops 9437184 | bytes 2124800 | tf_op jit(solution)/shard_map/kr,kh->rh/dot_general | solution.py:16
  6.8 1.0 %convolution_tanh_fusion.1 = f32[2048,256]{1,0:T(8,128)S(1)} fusion(f32[2048,256]{1,0:T(8,128)S(1)} %convolution_tanh_fusion.2, f32[256,256]{1,0:T(8,128)S(1)} %copy-done.3), kind=kOutput, calls=%fused_computation.5 | convolution fusion | flops 805306368 | bytes 4456448 | tf_op jit(solution)/shard_map/dot_general | solution.py:17
  7.8 1.0 %convolution_tanh_fusion = f32[2048,256]{1,0:T(8,128)S(1)} fusion(f32[2048,256]{1,0:T(8,128)S(1)} %convolution_tanh_fusion.1, f32[256,256]{1,0:T(8,128)S(1)} %copy-done.2), kind=kOutput, calls=%fused_computation.4 | convolution fusion | flops 805306368 | bytes 4456448 | tf_op jit(solution)/shard_map/dot_general | solution.py:18
  8.8 3.5 %fusion.1 = f32[256,3,128]{2,0,1:T(8,128)S(1)} fusion(f32[3,128,2048]{2,1,0:T(8,128)S(1)} %copy-done, f32[2048,256]{1,0:T(8,128)S(1)} %convolution_tanh_fusion), kind=kOutput, calls=%fused_computation.7 | convolution fusion | flops 1207959552 | bytes 5636096 | tf_op jit(solution)/shard_map/cfn,np->fcp/dot_general | solution.py:248
  12.4 2.8 %fusion = f32[2048,256]{1,0:T(8,128)S(1)} fusion(f32[128,3,256]{0,2,1:T(8,128)S(1)} %bitcast.54, f32[3,128,2048]{2,1,0:T(8,128)S(1)} %copy-done, f32[2048,256]{1,0:T(8,128)S(1)} %convolution_tanh_fusion), kind=kOutput, calls=%fused_computation.3 | convolution fusion | flops 1209532416 | bytes 7733248 | tf_op jit(solution)/shard_map/cfn,fcp->np/dot_general | solution.py:245
  15.2 0.6 convolution_multiply_fusion.3
  15.8 0.3 convolution_multiply_fusion.2
  16.2 0.3 fusion.3.refs_1_
  16.5 0.5 fusion.4.refs_2_
  17.1 2.1 %fusion.7.refs_5_ = f32[256,256]{1,0:T(8,128)S(1)} fusion(f32[2048,256]{1,0:T(8,128)S(1)} %convolution_tanh_fusion.1, f32[2048,256]{1,0:T(8,128)S(1)} %fusion), kind=kOutput, calls=%fused_computation.19 | convolution fusion | flops 805306368 | bytes 4456448 | tf_op jit(solution)/shard_map/dot_general | solution.py:25
  19.1 1.1 %convolution_multiply_fusion.1 = f32[2048,256]{1,0:T(8,128)S(1)} fusion(f32[2048,256]{1,0:T(8,128)S(1)} %fusion, f32[256,256]{1,0:T(8,128)S(1)} %copy-done.2, f32[2048,256]{1,0:T(8,128)S(1)} %convolution_tanh_fusion.1), kind=kOutput, calls=%fused_computation.1 | convolution fusion | flops 806879232 | bytes 6553600 | tf_op jit(solution)/shard_map/dot_general | solution.py:26
  20.2 1.9 %fusion.6.refs_4_ = f32[256,256]{1,0:T(8,128)S(1)} fusion(f32[2048,256]{1,0:T(8,128)S(1)} %convolution_tanh_fusion.2, f32[2048,256]{1,0:T(8,128)S(1)} %convolution_multiply_fusion.1), kind=kOutput, calls=%fused_computation.18 | convolution fusion | flops 805306368 | bytes 4456448 | tf_op jit(solution)/shard_map/dot_general | solution.py:29
  22.2 1.1 %convolution_multiply_fusion = f32[2048,256]{1,0:T(8,128)S(1)} fusion(f32[2048,256]{1,0:T(8,128)S(1)} %convolution_multiply_fusion.1, f32[256,256]{1,0:T(8,128)S(1)} %copy-done.3, f32[2048,256]{1,0:T(8,128)S(1)} %convolution_tanh_fusion.2), kind=kOutput, calls=%fused_computation | convolution fusion | flops 806879232 | bytes 6553600 | tf_op jit(solution)/shard_map/dot_general | solution.py:30
  23.2 0.6 convolution_bitcast_fusion.2.refs_3_
  23.8 34.2 %shard_map.136 = (f32[8,256]{1,0:T(8,128)S(1)}, f32[256,256]{1,0:T(8,128)S(1)}, f32[256,768]{1,0:T(8,128)S(1)}, f32[3,256]{1,0:T(4,128)S(1)}, f32[256,256]{1,0:T(8,128)S(1)}, /*index=5*/f32[256,256]{1,0:T(8,128)S(1)}) custom-call(f32[8,256]{1,0:T(8,128)S(1)} %convolution_bitcast_fusion.1.refs_0_, f32[256,256]{1,0:T(8,128)S(1)} %fusion.3.refs_1_, ...), custom_call_target="tpu_custom_call" | custom-call | tf_op jit(solution)/shard_map/pallas_call | solution.py:215
  58.0 0.6 copy.32
  58.6 0.7 %copy.33 = f32[256,256]{1,0:T(8,128)} copy(f32[256,256]{1,0:T(8,128)S(1)} %get-tuple-element.13) | data formatting | bytes 524288
  59.3 0.9 %copy.34 = f32[256,768]{1,0:T(8,128)} copy(f32[256,768]{1,0:T(8,128)S(1)} %get-tuple-element.14) | data formatting | bytes 1572864
  60.2 0.6 copy.35
  60.8 0.7 %copy.36 = f32[256,256]{1,0:T(8,128)} copy(f32[256,256]{1,0:T(8,128)S(1)} %get-tuple-element.16) | data formatting | bytes 524288
  61.5 0.7 %copy.37 = f32[256,256]{1,0:T(8,128)} copy(f32[256,256]{1,0:T(8,128)S(1)} %get-tuple-element.17) | data formatting | bytes 524288
  (15 shorter events, 0.2 us)
Async XLA Ops:
  0.6 8.2 %copy-start = (f32[3,128,2048]{2,1,0:T(8,128)S(1)}, f32[3,128,2048]{2,1,0:T(8,128)}, u32[]{:S(2)}) copy-start(f32[3,128,2048]{2,1,0:T(8,128)} %param.11) | copy-start | bytes 9437188
  0.6 6.1 %copy-start.3 = (f32[256,256]{1,0:T(8,128)S(1)}, f32[256,256]{1,0:T(8,128)}, u32[]{:S(2)}) copy-start(f32[256,256]{1,0:T(8,128)} %param.16) | copy-start | bytes 786436
  6.8 1.0 %copy-start.2 = (f32[256,256]{1,0:T(8,128)S(1)}, f32[256,256]{1,0:T(8,128)}, u32[]{:S(2)}) copy-start(f32[256,256]{1,0:T(8,128)} %param.17) | copy-start | bytes 786436
  12.3 2.8 %copy-start.1 = (f32[256,768]{1,0:T(8,128)S(1)}, f32[256,768]{1,0:T(8,128)}, u32[]{:S(2)}) copy-start(f32[256,768]{1,0:T(8,128)} %param.14) | copy-start | bytes 2359300
  12.4 3.4 %copy-start.4 = (f32[256,256]{1,0:T(8,128)S(1)}, f32[256,256]{1,0:T(8,128)}, u32[]{:S(2)}) copy-start(f32[256,256]{1,0:T(8,128)} %param.13) | copy-start | bytes 786436
  15.2 0.9 %copy-start.6 = (f32[8,128]{1,0:T(8,128)S(1)}, f32[8,128]{1,0:T(8,128)}, u32[]{:S(2)}) copy-start(f32[8,128]{1,0:T(8,128)} %param.9) | copy-start | bytes 12292
  22.1 1.1 %copy-start.5 = (f32[3,2048]{1,0:T(4,128)S(1)}, f32[3,2048]{1,0:T(4,128)}, u32[]{:S(2)}) copy-start(f32[3,2048]{1,0:T(4,128)} %param.10) | copy-start | bytes 73732

commit v3 on v2

--- a/solution.py
+++ b/solution.py
@@ -7,31 +7,21 @@
 from jax.experimental.pallas import tpu as pltpu
 from jax.sharding import PartitionSpec as P
 
-HIGH = lax.Precision.HIGH
 MESH = pl.DeviceIdType.MESH
 LANES = 128
 
 
-def layers_forward(inputs_t, first, second, out, last_tanh):
-    one = jnp.tanh(jnp.einsum("kr,kh->rh", inputs_t, first, precision=HIGH))
-    two = jnp.tanh(jnp.dot(one, second, precision=HIGH, preferred_element_type=jnp.float32))
-    top = jnp.dot(two, out, precision=HIGH, preferred_element_type=jnp.float32)
-    if last_tanh:
-        top = jnp.tanh(top)
-    return (one, two, top)
-
-
-def layers_backward(inputs_t, one, two, top_grad, second, out):
-    grad_out = jnp.dot(two.T, top_grad, precision=HIGH, preferred_element_type=jnp.float32)
-    dtwo = jnp.dot(top_grad, out.T, precision=HIGH, preferred_element_type=jnp.float32) * (
-        1.0 - two * two
+def split(value):
+    high = value.astype(jnp.bfloat16)
+    return high, (value - high.astype(jnp.float32)).astype(jnp.bfloat16)
+
+
+def dot(left, right, left_dim=1, right_dim=0):
+    lefts = jnp.concatenate([left[0], left[0], left[1]], axis=left_dim)
+    rights = jnp.concatenate([right[0], right[1], right[0]], axis=right_dim)
+    return lax.dot_general(
+        lefts, rights, (((left_dim,), (right_dim,)), ((), ())), preferred_element_type=jnp.float32
     )
-    grad_second = jnp.dot(one.T, dtwo, precision=HIGH, preferred_element_type=jnp.float32)
-    done = jnp.dot(dtwo, second.T, precision=HIGH, preferred_element_type=jnp.float32) * (
-        1.0 - one * one
-    )
-    grad_first = jnp.einsum("kr,rh->kh", inputs_t, done, precision=HIGH)
-    return (grad_first, grad_second, grad_out)
 
 
 class Plan:
@@ -39,7 +29,7 @@
         self.nf, self.nq = nf, nq
         unit = 8 * nf * nq
         units = -(-rows // (2 * unit))
-        a = max(1, (9 * units + 6) // 13)
+        a = max(1, (9 * units + 6) // 13) if units > 1 else 1
         self.ra, self.rb = a * unit, (units - a) * unit
         self.half = self.ra + self.rb
         self.total = 2 * self.half
@@ -120,7 +110,9 @@
     mine = c * plan.half
     other = (1 - c) * plan.half
 
-    go(acc.at[rows(other, plan.half)], core_in, sibling).wait_recv()
+    core = go(acc.at[rows(other, plan.half)], core_in, sibling)
+    yield
+    core.wait_recv()
     acc[rows(mine, plan.half), :] += core_in[...]
 
     base_a = mine + f * pa
@@ -134,6 +126,8 @@
         first_b = [
             go(acc.at[rows(mine + ra + d * pb, pb)], b1.at[k - 1], at_pts(d)) for k, d in pts_peers()
         ]
+
+    yield
 
     def add_up(into, start, size, slots, copies):
         value = acc[rows(start, size), :]
@@ -151,6 +145,8 @@
             go(acc.at[rows(base_b + d * sb, sb)], b2.at[k - 1], at_fab(d)) for k, d in fab_peers()
         ]
 
+    yield
+
     def give(start, size, peer):
         part = res.at[rows(start, size)]
         return go(part, part, peer)
@@ -161,6 +157,8 @@
     if has_b:
         add_up(res, own_b, sb, b2, second_b)
         third_b = [give(own_b, sb, at_fab(d)) for _, d in fab_peers()]
+
+    yield
 
     last = []
     for copy in third_a:
@@ -173,12 +171,14 @@
             copy.wait_recv()
         fourth_b = [give(base_b, pb, at_pts(d)) for _, d in pts_peers()]
         last.append(give(base_b, pb, sibling))
+    yield
     for k, copy in enumerate(fourth_a):
         copy.wait_recv()
         last.append(give(mine + lax.rem(f + nf - 1 - k, nf) * pa, pa, sibling))
     for k, copy in enumerate(fourth_b):
         copy.wait_recv()
         last.append(give(mine + ra + lax.rem(q + nq - 1 - k, nq) * pb, pb, sibling))
+    yield
     for copy in last:
         copy.wait_recv()
     for copy in started:
@@ -195,61 +195,235 @@
     return table, start
 
 
-def sum_kernel(plan, table, n, *refs):
-    ins, outs = refs[:n], refs[n : 2 * n]
-    acc, res, *rest = refs[2 * n :]
-    greet(plan)
-    acc[...] = jnp.zeros_like(acc)
-    for i, col, r, _, start in table:
-        acc[start : start + r, :] = ins[i][:, col : col + LANES]
-    sum_over_all(plan, acc, res, *rest)
-    for i, col, r, _, start in table:
-        outs[i][:, col : col + LANES] = res[start : start + r, :]
-
-
-def summed(grads, nf, nq):
-    shapes = [g.shape for g in grads]
-    table, rows = pieces(shapes)
-    plan = Plan(rows, nf, nq)
+def kernel(
+    plan_b,
+    plan_t,
+    table_b,
+    table_t,
+    fp_ref,
+    q_ref,
+    cot_ref,
+    b1_ref,
+    b2_ref,
+    b3_ref,
+    t1_ref,
+    t2_ref,
+    t3_ref,
+    out_b,
+    out_t,
+    cot,
+    cot_sem,
+    cot_hi,
+    cot_lo,
+    coef_hi,
+    coef_lo,
+    h1_hi,
+    h1_lo,
+    h2_hi,
+    h2_lo,
+    d1,
+    d2,
+    d3,
+    t2_split,
+    t3_split,
+    t2_turned,
+    t3_turned,
+    first_turned,
+    q_pad,
+    coef_grad,
+    g_first,
+    g_second,
+    g_out,
+    *comm,
+):
+    half = len(comm) // 2
+    acc_b, res_b, *rest_b = comm[:half]
+    acc_t, res_t, *rest_t = comm[half:]
+    load = pltpu.make_async_copy(cot_ref, cot, cot_sem)
+    load.start()
+
+    fab_local = fp_ref.shape[1]
+    points = q_ref.shape[1]
+    hidden, width = t3_ref.shape
+    step = min(points, 512)
+    steps = points // step
+    kq, kb = q_ref.shape[0], fp_ref.shape[0]
+
+    def keep(pair_ref, value):
+        pair_ref[0], pair_ref[1] = split(value)
+
+    def pair(ref):
+        return ref[0], ref[1]
+
+    q_pad[...] = jnp.zeros_like(q_pad)
+    q_pad[0:kq, :] = q_ref[...]
+    g_first[...] = jnp.zeros_like(g_first)
+    g_first[0:kq, :] = t1_ref[...]
+    first_turned[...] = g_first[...].T
+    keep(t2_split, t2_ref[...])
+    keep(t3_split, t3_ref[...])
+    keep(t2_turned, t2_ref[...].T)
+    keep(t3_turned, t3_ref[...].T)
+
+    fp_turned = fp_ref[...].T
+    pre = fp_turned[:, 0:1] * b1_ref[0:1, :]
+    for k in range(1, kb):
+        pre += fp_turned[:, k : k + 1] * b1_ref[k : k + 1, :]
+    hb1 = jnp.tanh(pre)
+    b2 = split(b2_ref[...])
+    hb2 = jnp.tanh(dot(split(hb1), b2))
+    b3 = split(b3_ref[...])
+    coef = dot(split(hb2), b3)
+    comps = coef.shape[1] // width
+    turned = jnp.concatenate([coef[:, c * width : (c + 1) * width].T for c in range(comps)], axis=1)
+    coef_hi[...], coef_lo[...] = split(turned)
+
+    coef_grad[...] = jnp.zeros_like(coef_grad)
+    load.wait()
+
+    def forward(i, carry):
+        xs = pl.ds(pl.multiple_of(i * step, step), step)
+        pre = first_turned[:, 0:1] * q_pad[0:1, xs]
+        for k in range(1, kq):
+            pre += first_turned[:, k : k + 1] * q_pad[k : k + 1, xs]
+        one = jnp.tanh(pre)
+        d1[:, xs] = 1.0 - one * one
+        one = split(one)
+        h1_hi[:, xs], h1_lo[:, xs] = one
+        two = jnp.tanh(dot(pair(t2_turned), one))
+        d2[:, xs] = 1.0 - two * two
+        two = split(two)
+        h2_hi[:, xs], h2_lo[:, xs] = two
+        basis = jnp.tanh(dot(pair(t3_turned), two))
+        d3[:, xs] = 1.0 - basis * basis
+        cots = split(cot[:, xs])
+        cot_hi[:, xs], cot_lo[:, xs] = cots
+        coef_grad[...] += dot(cots, split(basis), 1, 1)
+        return carry
+
+    lax.fori_loop(0, steps, forward, 0)
+
+    top = jnp.concatenate(
+        [coef_grad[c * fab_local : (c + 1) * fab_local, :] for c in range(comps)], axis=1
+    )
+    top = split(top)
+    gb3 = dot(split(hb2.T), top)
+    db2 = split(dot(top, b3, 1, 1) * (1.0 - hb2 * hb2))
+    gb2 = dot(split(hb1.T), db2)
+    for values, i in ((gb2, 0), (gb3, 1)):
+        for j, col, r, _, start in table_b:
+            if j == i:
+                acc_b[start : start + r, :] = values[:, col : col + LANES]
+    tail = table_b[-1][4] + table_b[-1][3]
+    if tail < plan_b.total:
+        acc_b[tail:, :] = jnp.zeros((plan_b.total - tail, LANES), jnp.float32)
+    greet(plan_b)
+    sum_b = sum_over_all(plan_b, acc_b, res_b, *rest_b)
+    next(sum_b)
+    db1 = dot(db2, b2, 1, 1) * (1.0 - hb1 * hb1)
+    gb1 = dot(split(fp_ref[...]), split(db1))
+
+    g_first[...] = jnp.zeros_like(g_first)
+    g_second[...] = jnp.zeros_like(g_second)
+    g_out[...] = jnp.zeros_like(g_out)
+
+    def backward(i):
+        xs = pl.ds(i * step, step)
+        three = dot((coef_hi[...], coef_lo[...]), (cot_hi[:, xs], cot_lo[:, xs])) * d3[:, xs]
+        three = split(three)
+        g_out[...] += dot((h2_hi[:, xs], h2_lo[:, xs]), three, 1, 1)
+        two = split(dot(pair(t3_split), three) * d2[:, xs])
+        g_second[...] += dot((h1_hi[:, xs], h1_lo[:, xs]), two, 1, 1)
+        one = split(dot(pair(t2_split), two) * d1[:, xs])
+        g_first[...] += dot(split(q_pad[:, xs]), one, 1, 1)
+
+    cuts = [0, steps // 4, steps // 2, steps]
+    for low, high in zip(cuts, cuts[1:]):
+        for i in range(low, high):
+            backward(i)
+        if high < steps:
+            next(sum_b)
+
+    parts = (gb1, g_first[...], g_second[...], g_out[...])
+    for i, col, r, kept, start in table_t:
+        acc_t[start : start + kept, :] = parts[i][0:kept, col : col + LANES]
+    tail = table_t[-1][4] + table_t[-1][3]
+    if tail < plan_t.total:
+        acc_t[tail:, :] = jnp.zeros((plan_t.total - tail, LANES), jnp.float32)
+    sums = [sum_over_all(plan_t, acc_t, res_t, *rest_t), sum_b]
+    while sums:
+        for one in list(sums):
+            if next(one, True):
+                sums.remove(one)
+    out_b[...] = res_b[...]
+    out_t[...] = res_t[...]
+
+
+def unpack(tables, shapes, flat_b, flat_t, *outs):
+    for flat, table, group in zip((flat_b, flat_t), tables, shapes):
+        for i, col, r, _, start in table:
+            outs[group[i]][:, col : col + LANES] = flat[start : start + r, :]
+
+
+def local(nf, nq, fabric_params, query_points, cotangent, b1, b2, b3, t1, t2, t3):
+    comps, fab_local, points = cotangent.shape
+    cot = cotangent.reshape(comps * fab_local, points)
+    shapes = [w.shape for w in (b1, b2, b3, t1, t2, t3)]
+    group_b, group_t = (1, 2), (0, 3, 4, 5)
+    table_b, rows_b = pieces([shapes[i] for i in group_b])
+    table_t, rows_t = pieces([shapes[i] for i in group_t])
+    plan_b, plan_t = Plan(rows_b, nf, nq), Plan(rows_t, nf, nq)
+    hidden, width = t3.shape
     vmem = pl.BlockSpec(memory_space=pltpu.VMEM)
-    return pl.pallas_call(
-        functools.partial(sum_kernel, plan, table, len(grads)),
-        out_shape=[jax.ShapeDtypeStruct(s, jnp.float32) for s in shapes],
-        in_specs=[vmem] * len(grads),
-        out_specs=[vmem] * len(grads),
-        scratch_shapes=plan.scratch(),
+    f32, bf16 = jnp.float32, jnp.bfloat16
+    rows = comps * fab_local
+    flat_b, flat_t = pl.pallas_call(
+        functools.partial(kernel, plan_b, plan_t, table_b, table_t),
+        out_shape=[
+            jax.ShapeDtypeStruct((plan_b.total, LANES), f32),
+            jax.ShapeDtypeStruct((plan_t.total, LANES), f32),
+        ],
+        in_specs=[vmem, vmem, pl.BlockSpec(memory_space=pl.ANY)] + [vmem] * 6,
+        out_specs=[vmem] * 2,
+        scratch_shapes=[
+            pltpu.VMEM((rows, points), f32),
+            pltpu.SemaphoreType.DMA,
+            pltpu.VMEM((rows, points), bf16),
+            pltpu.VMEM((rows, points), bf16),
+            pltpu.VMEM((width, rows), bf16),
+            pltpu.VMEM((width, rows), bf16),
+            pltpu.VMEM((hidden, points), bf16),
+            pltpu.VMEM((hidden, points), bf16),
+            pltpu.VMEM((hidden, points), bf16),
+            pltpu.VMEM((hidden, points), bf16),
+            pltpu.VMEM((hidden, points), f32),
+            pltpu.VMEM((hidden, points), f32),
+            pltpu.VMEM((width, points), f32),
+            pltpu.VMEM((2,) + t2.shape, bf16),
+            pltpu.VMEM((2,) + t3.shape, bf16),
+            pltpu.VMEM((2,) + t2.shape[::-1], bf16),
+            pltpu.VMEM((2,) + t3.shape[::-1], bf16),
+            pltpu.VMEM((hidden, 8), f32),
+            pltpu.VMEM((8, points), f32),
+            pltpu.VMEM((rows, width), f32),
+            pltpu.VMEM((8, hidden), f32),
+            pltpu.VMEM(t2.shape, f32),
+            pltpu.VMEM(t3.shape, f32),
+        ]
+        + plan_b.scratch()
+        + plan_t.scratch(),
         compiler_params=pltpu.CompilerParams(
-            collective_id=0, has_side_effects=True, vmem_limit_bytes=40 * 1024 * 1024
+            collective_id=0, has_side_effects=True, vmem_limit_bytes=50 * 1024 * 1024
         ),
-    )(*grads)
-
-
-def local(
-    nf,
-    nq,
-    fabric_params,
-    query_points,
-    cotangent,
-    branch_first,
-    branch_second,
-    branch_out,
-    trunk_first,
-    trunk_second,
-    trunk_out,
-):
-    hb1, hb2, coef = layers_forward(fabric_params, branch_first, branch_second, branch_out, False)
-    ht1, ht2, basis = layers_forward(query_points, trunk_first, trunk_second, trunk_out, True)
-    fab_local = coef.shape[0]
-    width = basis.shape[1]
-    coef_split = coef.reshape(fab_local, 3, width)
-    basis_grad = jnp.einsum("cfn,fcp->np", cotangent, coef_split, precision=HIGH)
-    top_grad = basis_grad * (1.0 - basis * basis)
-    local_trunk = layers_backward(query_points, ht1, ht2, top_grad, trunk_second, trunk_out)
-    coef_grad = jnp.einsum("cfn,np->fcp", cotangent, basis, precision=HIGH).reshape(
-        fab_local, 3 * width
+    )(fabric_params, query_points, cot, b1, b2, b3, t1, t2, t3)
+    return tuple(
+        pl.pallas_call(
+            functools.partial(unpack, (table_b, table_t), (group_b, group_t)),
+            out_shape=[jax.ShapeDtypeStruct(s, f32) for s in shapes],
+            in_specs=[vmem] * 2,
+            out_specs=[vmem] * 6,
+        )(flat_b, flat_t)
     )
-    local_branch = layers_backward(fabric_params, hb1, hb2, coef_grad, branch_second, branch_out)
-    return tuple(summed(local_branch + local_trunk, nf, nq))
 
 
 def solution(mesh):

time: 62.4 us -> 59.9 us (0.960)
  matrix products: 22.9 us -> 0 us
  Pallas kernels: 34.2 us -> 50.1 us
  local copies, waits for them, and re-layouts: 4.22 us -> 8.64 us
    dot_general x18 -> x0, matrix products: 22.9 us -> none  [the longest x1 3.52 us: local(): jnp.einsum('cfn,np->fcp', cotangent, basis, precision=HIGH)]
    pallas_call x1 -> x2, Pallas kernels: 34.2 us -> 50.1 us  [the longest x1 47.6 us: local(): pl.pallas_call(functools.partial(kernel, plan_b, plan_t, table_b, table_t...]
    unnamed x20, local copies, waits for them, and re-layouts: 4.22 us -> 8.64 us
where the time goes in v3:
time: 59.9 us; the launch traced here: 59.5 us
  Pallas kernels  50.1 us (84%)
  local copies, waits for them, and re-layouts  8.64 us (14%)
  between operations  0.67 us (1%)
    pallas_call x1, Pallas kernels, local(): pl.pallas_call(functools.partial(kernel, plan_b, plan_t, table_b, table_t...  47.6 us
    unnamed x20, local copies, waits for them, and re-layouts  8.64 us
    pallas_call x1, Pallas kernels, local(): pl.pallas_call(functools.partial(unpack, (table_b, table_t), (group_b, gr...  2.56 us

profile of v3, /device:TPU:0, one launch (start us, length us, event | category | flops | bytes accessed | tf_op | source)
XLA Modules:
  0.0 59.5 jit_solution(15107331049783387852)
XLA Ops:
  0.6 0.0 copy-start.1
  0.6 1.1 %copy-done.1 = f32[256,768]{1,0:T(8,128)S(1)} copy-done((f32[256,768]{1,0:T(8,128)S(1)}, f32[256,768]{1,0:T(8,128)}, u32[]{:S(2)}) %copy-start.1) | copy-done | bytes 786456
  1.8 0.0 copy-start.3
  1.8 0.9 %copy-done.3 = f32[256,256]{1,0:T(8,128)S(1)} copy-done((f32[256,256]{1,0:T(8,128)S(1)}, f32[256,256]{1,0:T(8,128)}, u32[]{:S(2)}) %copy-start.3) | copy-done | bytes 262168
  2.7 0.0 copy-start.4
  2.7 0.9 %copy-done.4 = f32[256,256]{1,0:T(8,128)S(1)} copy-done((f32[256,256]{1,0:T(8,128)S(1)}, f32[256,256]{1,0:T(8,128)}, u32[]{:S(2)}) %copy-start.4) | copy-done | bytes 262168
  3.7 0.0 copy-start.5
  3.7 0.9 %copy-done.5 = f32[256,256]{1,0:T(8,128)S(1)} copy-done((f32[256,256]{1,0:T(8,128)S(1)}, f32[256,256]{1,0:T(8,128)}, u32[]{:S(2)}) %copy-start.5) | copy-done | bytes 262168
  4.6 0.0 copy-start.6
  4.6 0.8 %copy-done.6 = f32[3,2048]{1,0:T(4,128)S(1)} copy-done((f32[3,2048]{1,0:T(4,128)S(1)}, f32[3,2048]{1,0:T(4,128)}, u32[]{:S(2)}) %copy-start.6) | copy-done | bytes 24600
  5.4 0.0 copy-start.7
  5.4 0.7 %copy-done.7 = f32[8,256]{1,0:T(8,128)S(1)} copy-done((f32[8,256]{1,0:T(8,128)S(1)}, f32[8,256]{1,0:T(8,128)}, u32[]{:S(2)}) %copy-start.7) | copy-done | bytes 8216
  6.1 0.0 copy-start.8
  6.1 0.7 %copy-done.8 = f32[8,128]{1,0:T(8,128)S(1)} copy-done((f32[8,128]{1,0:T(8,128)S(1)}, f32[8,128]{1,0:T(8,128)}, u32[]{:S(2)}) %copy-start.8) | copy-done | bytes 4120
  6.8 0.0 copy-start.9
  6.8 0.7 %copy-done.9 = f32[3,256]{1,0:T(4,128)S(1)} copy-done((f32[3,256]{1,0:T(4,128)S(1)}, f32[3,256]{1,0:T(4,128)}, u32[]{:S(2)}) %copy-start.9) | copy-done | bytes 3096
  7.5 47.6 %shard_map.136 = (f32[2048,128]{1,0:T(8,128)S(1)}, f32[1280,128]{1,0:T(8,128)S(1)}) custom-call(f32[8,128]{1,0:T(8,128)S(1)} %copy-done.8, f32[3,2048]{1,0:T(4,128)S(1)} %copy-done.6, f32[384,2048]{1,0:T(8,128)} %bitcast.1, f32[8,256]{1,0:T(8,128)S(1)} %copy-done.7, f32[256,256]{1,0:T(8,128)S(1)} %copy-done.3, f32[256,768]{1,0:T(8,128)S(1)} %copy-done.1, ...), custom_call_target="tpu_custom_call" | custom-call | tf_op jit(solution)/shard_map/pallas_call | solution.py:380
  55.0 0.0 copy-start
  55.1 1.0 %copy-done = f32[2048,128]{1,0:T(8,128)} copy-done((f32[2048,128]{1,0:T(8,128)}, f32[2048,128]{1,0:T(8,128)S(1)}, u32[]{:S(2)}) %copy-start) | copy-done | bytes 1048600
  56.0 0.0 copy-start.2
  56.0 0.9 %copy-done.2 = f32[1280,128]{1,0:T(8,128)} copy-done((f32[1280,128]{1,0:T(8,128)}, f32[1280,128]{1,0:T(8,128)S(1)}, u32[]{:S(2)}) %copy-start.2) | copy-done | bytes 655384
  56.9 2.6 %shard_map.137 = (f32[8,256]{1,0:T(8,128)}, f32[256,256]{1,0:T(8,128)}, f32[256,768]{1,0:T(8,128)}, f32[3,256]{1,0:T(4,128)}, f32[256,256]{1,0:T(8,128)}, /*index=5*/f32[256,256]{1,0:T(8,128)}) custom-call(f32[2048,128]{1,0:T(8,128)} %copy-done, f32[1280,128]{1,0:T(8,128)} %copy-done.2), custom_call_target="tpu_custom_call" | custom-call | tf_op jit(solution)/shard_map/pallas_call | solution.py:420
Async XLA Ops:
  0.6 1.1 %copy-start.1 = (f32[256,768]{1,0:T(8,128)S(1)}, f32[256,768]{1,0:T(8,128)}, u32[]{:S(2)}) copy-start(f32[256,768]{1,0:T(8,128)} %b3_ref.1) | copy-start | bytes 2359300
  1.8 0.9 %copy-start.3 = (f32[256,256]{1,0:T(8,128)S(1)}, f32[256,256]{1,0:T(8,128)}, u32[]{:S(2)}) copy-start(f32[256,256]{1,0:T(8,128)} %b2_ref.1) | copy-start | bytes 786436
  2.7 0.9 %copy-start.4 = (f32[256,256]{1,0:T(8,128)S(1)}, f32[256,256]{1,0:T(8,128)}, u32[]{:S(2)}) copy-start(f32[256,256]{1,0:T(8,128)} %t2_ref.1) | copy-start | bytes 786436
  3.7 0.9 %copy-start.5 = (f32[256,256]{1,0:T(8,128)S(1)}, f32[256,256]{1,0:T(8,128)}, u32[]{:S(2)}) copy-start(f32[256,256]{1,0:T(8,128)} %t3_ref.1) | copy-start | bytes 786436
  4.6 0.8 %copy-start.6 = (f32[3,2048]{1,0:T(4,128)S(1)}, f32[3,2048]{1,0:T(4,128)}, u32[]{:S(2)}) copy-start(f32[3,2048]{1,0:T(4,128)} %q_ref.1) | copy-start | bytes 73732
  5.4 0.7 %copy-start.7 = (f32[8,256]{1,0:T(8,128)S(1)}, f32[8,256]{1,0:T(8,128)}, u32[]{:S(2)}) copy-start(f32[8,256]{1,0:T(8,128)} %b1_ref.1) | copy-start | bytes 24580
  6.1 0.7 %copy-start.8 = (f32[8,128]{1,0:T(8,128)S(1)}, f32[8,128]{1,0:T(8,128)}, u32[]{:S(2)}) copy-start(f32[8,128]{1,0:T(8,128)} %fp_ref.1) | copy-start | bytes 12292
  6.8 0.7 %copy-start.9 = (f32[3,256]{1,0:T(4,128)S(1)}, f32[3,256]{1,0:T(4,128)}, u32[]{:S(2)}) copy-start(f32[3,256]{1,0:T(4,128)} %t1_ref.1) | copy-start | bytes 9220
  55.0 1.0 %copy-start = (f32[2048,128]{1,0:T(8,128)}, f32[2048,128]{1,0:T(8,128)S(1)}, u32[]{:S(2)}) copy-start(f32[2048,128]{1,0:T(8,128)S(1)} %get-tuple-element.8.flat_b) | copy-start | bytes 3145732
  56.0 0.9 %copy-start.2 = (f32[1280,128]{1,0:T(8,128)}, f32[1280,128]{1,0:T(8,128)S(1)}, u32[]{:S(2)}) copy-start(f32[1280,128]{1,0:T(8,128)S(1)} %get-tuple-element.9.flat_t) | copy-start | bytes 1966084

commit v4 on v3

--- a/solution.py
+++ b/solution.py
@@ -66,7 +66,10 @@
     peers += [(f, 2 * lax.rem(q + k, plan.nq) + c) for k in range(1, plan.nq)]
     for peer in peers:
         pl.semaphore_signal(barrier, inc=1, device_id=peer, device_id_type=MESH)
-    pl.semaphore_wait(barrier, len(peers))
+
+
+def met(plan):
+    pl.semaphore_wait(pltpu.get_barrier_semaphore(), plan.nf + plan.nq - 1)
 
 
 def sum_over_all(plan, acc, res, core_in, a1, b1, a2, b2, send, recv):
@@ -200,19 +203,37 @@
     plan_t,
     table_b,
     table_t,
+    *refs,
+):
+    given, outs, held = refs[:9], refs[9:11], refs[11:20]
+    loads = [
+        pltpu.make_async_copy(src, dst, refs[20].at[i])
+        for i, (src, dst) in enumerate(zip(given, held))
+    ]
+    for i in (6, 1, 7, 8, 0, 3, 4, 5, 2):
+        loads[i].start()
+    greet(plan_b)
+    compute(plan_b, plan_t, table_b, table_t, loads, *outs, refs[21], *held, *refs[22:])
+
+
+def compute(
+    plan_b,
+    plan_t,
+    table_b,
+    table_t,
+    loads,
+    out_b,
+    out_t,
+    out_sem,
     fp_ref,
     q_ref,
-    cot_ref,
+    cot,
     b1_ref,
     b2_ref,
     b3_ref,
     t1_ref,
     t2_ref,
     t3_ref,
-    out_b,
-    out_t,
-    cot,
-    cot_sem,
     cot_hi,
     cot_lo,
     coef_hi,
@@ -239,9 +260,9 @@
     half = len(comm) // 2
     acc_b, res_b, *rest_b = comm[:half]
     acc_t, res_t, *rest_t = comm[half:]
-    load = pltpu.make_async_copy(cot_ref, cot, cot_sem)
-    load.start()
-
+
+    for i in (6, 1, 7, 8):
+        loads[i].wait()
     fab_local = fp_ref.shape[1]
     points = q_ref.shape[1]
     hidden, width = t3_ref.shape
@@ -264,6 +285,9 @@
     keep(t3_split, t3_ref[...])
     keep(t2_turned, t2_ref[...].T)
     keep(t3_turned, t3_ref[...].T)
+
+    for i in (0, 3, 4, 5):
+        loads[i].wait()
 
     fp_turned = fp_ref[...].T
     pre = fp_turned[:, 0:1] * b1_ref[0:1, :]
@@ -279,7 +303,7 @@
     coef_hi[...], coef_lo[...] = split(turned)
 
     coef_grad[...] = jnp.zeros_like(coef_grad)
-    load.wait()
+    loads[2].wait()
 
     def forward(i, carry):
         xs = pl.ds(pl.multiple_of(i * step, step), step)
@@ -317,7 +341,7 @@
     tail = table_b[-1][4] + table_b[-1][3]
     if tail < plan_b.total:
         acc_b[tail:, :] = jnp.zeros((plan_b.total - tail, LANES), jnp.float32)
-    greet(plan_b)
+    met(plan_b)
     sum_b = sum_over_all(plan_b, acc_b, res_b, *rest_b)
     next(sum_b)
     db1 = dot(db2, b2, 1, 1) * (1.0 - hb1 * hb1)
@@ -337,7 +361,7 @@
         one = split(dot(pair(t2_split), two) * d1[:, xs])
         g_first[...] += dot(split(q_pad[:, xs]), one, 1, 1)
 
-    cuts = [0, steps // 4, steps // 2, steps]
+    cuts = [0, steps // 4, steps]
     for low, high in zip(cuts, cuts[1:]):
         for i in range(low, high):
             backward(i)
@@ -351,18 +375,41 @@
     if tail < plan_t.total:
         acc_t[tail:, :] = jnp.zeros((plan_t.total - tail, LANES), jnp.float32)
     sums = [sum_over_all(plan_t, acc_t, res_t, *rest_t), sum_b]
-    while sums:
-        for one in list(sums):
-            if next(one, True):
-                sums.remove(one)
-    out_b[...] = res_b[...]
-    out_t[...] = res_t[...]
-
-
-def unpack(tables, shapes, flat_b, flat_t, *outs):
-    for flat, table, group in zip((flat_b, flat_t), tables, shapes):
+    stores = (
+        pltpu.make_async_copy(res_t, out_t, out_sem.at[0]),
+        pltpu.make_async_copy(res_b, out_b, out_sem.at[1]),
+    )
+    while any(sums):
+        for i, one in enumerate(sums):
+            if one is not None and next(one, True):
+                stores[i].start()
+                sums[i] = None
+    for store in stores:
+        store.wait()
+
+
+def unpack(tables, groups, flat_b, flat_t, *refs):
+    outs, small, sems = refs[:6], refs[6], refs[7]
+    first = pltpu.make_async_copy(flat_t.at[pl.ds(0, small.shape[0])], small, sems.at[0])
+    first.start()
+    copies = []
+    for flat, table, group in zip((flat_b, flat_t), tables, groups):
         for i, col, r, _, start in table:
-            outs[group[i]][:, col : col + LANES] = flat[start : start + r, :]
+            if group[i] not in (0, 3):
+                copies.append(
+                    pltpu.make_async_copy(
+                        flat.at[pl.ds(start, r)],
+                        outs[group[i]].at[:, pl.ds(col, LANES)],
+                        sems.at[1 + len(copies)],
+                    )
+                )
+                copies[-1].start()
+    first.wait()
+    for i, col, r, _, start in tables[1]:
+        if groups[1][i] in (0, 3):
+            outs[groups[1][i]][:, col : col + LANES] = small[start : start + r, :]
+    for copy in copies:
+        copy.wait()
 
 
 def local(nf, nq, fabric_params, query_points, cotangent, b1, b2, b3, t1, t2, t3):
@@ -375,6 +422,8 @@
     plan_b, plan_t = Plan(rows_b, nf, nq), Plan(rows_t, nf, nq)
     hidden, width = t3.shape
     vmem = pl.BlockSpec(memory_space=pltpu.VMEM)
+    hbm = pl.BlockSpec(memory_space=pl.ANY)
+    small = sum(kept for i, _, _, kept, _ in table_t if group_t[i] in (0, 3))
     f32, bf16 = jnp.float32, jnp.bfloat16
     rows = comps * fab_local
     flat_b, flat_t = pl.pallas_call(
@@ -383,11 +432,15 @@
             jax.ShapeDtypeStruct((plan_b.total, LANES), f32),
             jax.ShapeDtypeStruct((plan_t.total, LANES), f32),
         ],
-        in_specs=[vmem, vmem, pl.BlockSpec(memory_space=pl.ANY)] + [vmem] * 6,
-        out_specs=[vmem] * 2,
+        in_specs=[hbm] * 9,
+        out_specs=[hbm] * 2,
         scratch_shapes=[
-            pltpu.VMEM((rows, points), f32),
-            pltpu.SemaphoreType.DMA,
+            *[
+                pltpu.VMEM(x.shape, f32)
+                for x in (fabric_params, query_points, cot, b1, b2, b3, t1, t2, t3)
+            ],
+            pltpu.SemaphoreType.DMA((9,)),
+            pltpu.SemaphoreType.DMA((2,)),
             pltpu.VMEM((rows, points), bf16),
             pltpu.VMEM((rows, points), bf16),
             pltpu.VMEM((width, rows), bf16),
@@ -420,8 +473,12 @@
         pl.pallas_call(
             functools.partial(unpack, (table_b, table_t), (group_b, group_t)),
             out_shape=[jax.ShapeDtypeStruct(s, f32) for s in shapes],
-            in_specs=[vmem] * 2,
-            out_specs=[vmem] * 6,
+            in_specs=[hbm] * 2,
+            out_specs=[vmem if i in (0, 3) else hbm for i in range(6)],
+            scratch_shapes=[
+                pltpu.VMEM((small, LANES), f32),
+                pltpu.SemaphoreType.DMA((1 + len(table_b) + len(table_t),)),
+            ],
         )(flat_b, flat_t)
     )
 

time: 59.9 us -> 102 us (1.70)
  Pallas kernels: 50.1 us -> 92.6 us
    pallas_call x1, Pallas kernels: 2.56 us -> 49.5 us  [local(): pl.pallas_call(functools.partial(unpack, (table_b, table_t), (group_b, gr...]
    pallas_call x1, Pallas kernels: 47.6 us -> 43.1 us  [local(): pl.pallas_call(functools.partial(kernel, plan_b, plan_t, table_b, table_t...]
where the time goes in v4:
time: 102 us
  Pallas kernels  92.6 us (91%)
  local copies, waits for them, and re-layouts  8.64 us (8%)
    pallas_call x1, Pallas kernels, local(): pl.pallas_call(functools.partial(unpack, (table_b, table_t), (group_b, gr...  49.5 us
    pallas_call x1, Pallas kernels, local(): pl.pallas_call(functools.partial(kernel, plan_b, plan_t, table_b, table_t...  43.1 us
    unnamed x20, local copies, waits for them, and re-layouts  8.64 us

profile of v4, /device:TPU:0, one launch (start us, length us, event | category | flops | bytes accessed | tf_op | source)
XLA Modules:
  0.0 101.9 jit_solution(5633316867439917596)
XLA Ops:
  0.6 0.0 copy-start.1
  0.6 1.1 %copy-done.1 = f32[256,768]{1,0:T(8,128)S(1)} copy-done((f32[256,768]{1,0:T(8,128)S(1)}, f32[256,768]{1,0:T(8,128)}, u32[]{:S(2)}) %copy-start.1) | copy-done | bytes 786456
  1.8 0.0 copy-start.3
  1.8 0.9 copy-done.3
  2.7 0.0 copy-start.4
  2.7 0.9 copy-done.4
  3.7 0.0 copy-start.5
  3.7 0.9 copy-done.5
  4.6 0.0 copy-start.6
  4.6 0.8 copy-done.6
  5.4 0.0 copy-start.7
  5.4 0.7 copy-done.7
  6.1 0.0 copy-start.8
  6.1 0.7 copy-done.8
  6.8 0.0 copy-start.9
  6.8 0.7 copy-done.9
  7.5 43.1 %shard_map.136 = (f32[2048,128]{1,0:T(8,128)S(1)}, f32[1280,128]{1,0:T(8,128)S(1)}) custom-call(f32[8,128]{1,0:T(8,128)S(1)} %copy-done.8, f32[3,2048]{1,0:T(4,128)S(1)} %copy-done.6, f32[384,2048]{1,0:T(8,128)} %bitcast.1, f32[8,256]{1,0:T(8,128)S(1)} %copy-done.7, f32[256,256]{1,0:T(8,128)S(1)} %copy-done.3, f32[256,768]{1,0:T(8,128)S(1)} %copy-done.1, ...), custom_call_target="tpu_custom_call" | custom-call | tf_op jit(solution)/shard_map/pallas_call | solution.py:429
  50.5 0.0 copy-start
  50.6 1.0 copy-done
  51.5 0.0 copy-start.2
  51.5 0.9 copy-done.2
  52.4 49.5 %shard_map.137 = (f32[8,256]{1,0:T(8,128)}, f32[256,256]{1,0:T(8,128)}, f32[256,768]{1,0:T(8,128)}, f32[3,256]{1,0:T(4,128)}, f32[256,256]{1,0:T(8,128)}, /*index=5*/f32[256,256]{1,0:T(8,128)}) custom-call(f32[2048,128]{1,0:T(8,128)} %copy-done, f32[1280,128]{1,0:T(8,128)} %copy-done.2), custom_call_target="tpu_custom_call" | custom-call | tf_op jit(solution)/shard_map/pallas_call | solution.py:473
Async XLA Ops:
  0.6 1.1 %copy-start.1 = (f32[256,768]{1,0:T(8,128)S(1)}, f32[256,768]{1,0:T(8,128)}, u32[]{:S(2)}) copy-start(f32[256,768]{1,0:T(8,128)} %refs_5_.1) | copy-start | bytes 2359300
  1.8 0.9 copy-start.3
  2.7 0.9 copy-start.4
  3.7 0.9 copy-start.5
  4.6 0.8 copy-start.6
  5.4 0.7 copy-start.7
  6.1 0.7 copy-start.8
  6.8 0.7 copy-start.9
  50.5 1.0 copy-start
  51.5 0.9 copy-start.2

commit v5 on v4

--- a/solution.py
+++ b/solution.py
@@ -389,27 +389,14 @@
 
 
 def unpack(tables, groups, flat_b, flat_t, *refs):
-    outs, small, sems = refs[:6], refs[6], refs[7]
-    first = pltpu.make_async_copy(flat_t.at[pl.ds(0, small.shape[0])], small, sems.at[0])
-    first.start()
-    copies = []
-    for flat, table, group in zip((flat_b, flat_t), tables, groups):
+    outs, held, sems = refs[:6], refs[6:8], refs[8]
+    loads = [pltpu.make_async_copy((flat_b, flat_t)[i], held[i], sems.at[i]) for i in range(2)]
+    for load in loads:
+        load.start()
+    for load, flat, table, group in zip(loads, held, tables, groups):
+        load.wait()
         for i, col, r, _, start in table:
-            if group[i] not in (0, 3):
-                copies.append(
-                    pltpu.make_async_copy(
-                        flat.at[pl.ds(start, r)],
-                        outs[group[i]].at[:, pl.ds(col, LANES)],
-                        sems.at[1 + len(copies)],
-                    )
-                )
-                copies[-1].start()
-    first.wait()
-    for i, col, r, _, start in tables[1]:
-        if groups[1][i] in (0, 3):
-            outs[groups[1][i]][:, col : col + LANES] = small[start : start + r, :]
-    for copy in copies:
-        copy.wait()
+            outs[group[i]][:, col : col + LANES] = flat[start : start + r, :]
 
 
 def local(nf, nq, fabric_params, query_points, cotangent, b1, b2, b3, t1, t2, t3):
@@ -422,8 +409,7 @@
     plan_b, plan_t = Plan(rows_b, nf, nq), Plan(rows_t, nf, nq)
     hidden, width = t3.shape
     vmem = pl.BlockSpec(memory_space=pltpu.VMEM)
-    hbm = pl.BlockSpec(memory_space=pl.ANY)
-    small = sum(kept for i, _, _, kept, _ in table_t if group_t[i] in (0, 3))
+    hbm = pl.BlockSpec(memory_space=pltpu.HBM)
     f32, bf16 = jnp.float32, jnp.bfloat16
     rows = comps * fab_local
     flat_b, flat_t = pl.pallas_call(
@@ -474,10 +460,11 @@
             functools.partial(unpack, (table_b, table_t), (group_b, group_t)),
             out_shape=[jax.ShapeDtypeStruct(s, f32) for s in shapes],
             in_specs=[hbm] * 2,
-            out_specs=[vmem if i in (0, 3) else hbm for i in range(6)],
+            out_specs=[vmem] * 6,
             scratch_shapes=[
-                pltpu.VMEM((small, LANES), f32),
-                pltpu.SemaphoreType.DMA((1 + len(table_b) + len(table_t),)),
+                pltpu.VMEM((plan_b.total, LANES), f32),
+                pltpu.VMEM((plan_t.total, LANES), f32),
+                pltpu.SemaphoreType.DMA((2,)),
             ],
         )(flat_b, flat_t)
     )

time: 102 us -> 55.4 us (0.54)
  Pallas kernels: 92.6 us -> 45.6 us
    pallas_call x1, Pallas kernels: 49.5 us -> 2.56 us  [local(): pl.pallas_call(functools.partial(unpack, (table_b, table_t), (group_b, gr...]
where the time goes in v5:
time: 55.4 us; the launch traced here: 55 us
  Pallas kernels  45.6 us (82%)
  local copies, waits for them, and re-layouts  8.64 us (16%)
  between operations  0.67 us (1%)
    pallas_call x1, Pallas kernels, local(): pl.pallas_call(functools.partial(kernel, plan_b, plan_t, table_b, table_t...  43.1 us
    unnamed x20, local copies, waits for them, and re-layouts  8.64 us
    pallas_call x1, Pallas kernels, local(): pl.pallas_call(functools.partial(unpack, (table_b, table_t), (group_b, gr...  2.56 us

profile of v5, /device:TPU:0, one launch (start us, length us, event | category | flops | bytes accessed | tf_op | source)
XLA Modules:
  0.0 55.0 jit_solution(17064204616490320593)
XLA Ops:
  0.6 0.0 copy-start.1
  0.6 1.1 %copy-done.1 = f32[256,768]{1,0:T(8,128)S(1)} copy-done((f32[256,768]{1,0:T(8,128)S(1)}, f32[256,768]{1,0:T(8,128)}, u32[]{:S(2)}) %copy-start.1) | copy-done | bytes 786456
  1.8 0.0 copy-start.3
  1.8 0.9 %copy-done.3 = f32[256,256]{1,0:T(8,128)S(1)} copy-done((f32[256,256]{1,0:T(8,128)S(1)}, f32[256,256]{1,0:T(8,128)}, u32[]{:S(2)}) %copy-start.3) | copy-done | bytes 262168
  2.7 0.0 copy-start.4
  2.7 0.9 %copy-done.4 = f32[256,256]{1,0:T(8,128)S(1)} copy-done((f32[256,256]{1,0:T(8,128)S(1)}, f32[256,256]{1,0:T(8,128)}, u32[]{:S(2)}) %copy-start.4) | copy-done | bytes 262168
  3.7 0.0 copy-start.5
  3.7 0.9 %copy-done.5 = f32[256,256]{1,0:T(8,128)S(1)} copy-done((f32[256,256]{1,0:T(8,128)S(1)}, f32[256,256]{1,0:T(8,128)}, u32[]{:S(2)}) %copy-start.5) | copy-done | bytes 262168
  4.6 0.0 copy-start.6
  4.6 0.8 %copy-done.6 = f32[3,2048]{1,0:T(4,128)S(1)} copy-done((f32[3,2048]{1,0:T(4,128)S(1)}, f32[3,2048]{1,0:T(4,128)}, u32[]{:S(2)}) %copy-start.6) | copy-done | bytes 24600
  5.4 0.0 copy-start.7
  5.4 0.7 %copy-done.7 = f32[8,256]{1,0:T(8,128)S(1)} copy-done((f32[8,256]{1,0:T(8,128)S(1)}, f32[8,256]{1,0:T(8,128)}, u32[]{:S(2)}) %copy-start.7) | copy-done | bytes 8216
  6.1 0.0 copy-start.8
  6.1 0.7 %copy-done.8 = f32[8,128]{1,0:T(8,128)S(1)} copy-done((f32[8,128]{1,0:T(8,128)S(1)}, f32[8,128]{1,0:T(8,128)}, u32[]{:S(2)}) %copy-start.8) | copy-done | bytes 4120
  6.8 0.0 copy-start.9
  6.8 0.7 %copy-done.9 = f32[3,256]{1,0:T(4,128)S(1)} copy-done((f32[3,256]{1,0:T(4,128)S(1)}, f32[3,256]{1,0:T(4,128)}, u32[]{:S(2)}) %copy-start.9) | copy-done | bytes 3096
  7.5 43.1 %shard_map.136 = (f32[2048,128]{1,0:T(8,128)S(1)}, f32[1280,128]{1,0:T(8,128)S(1)}) custom-call(f32[8,128]{1,0:T(8,128)S(1)} %copy-done.8, f32[3,2048]{1,0:T(4,128)S(1)} %copy-done.6, f32[384,2048]{1,0:T(8,128)} %bitcast.1, f32[8,256]{1,0:T(8,128)S(1)} %copy-done.7, f32[256,256]{1,0:T(8,128)S(1)} %copy-done.3, f32[256,768]{1,0:T(8,128)S(1)} %copy-done.1, ...), custom_call_target="tpu_custom_call" | custom-call | tf_op jit(solution)/shard_map/pallas_call | solution.py:415
  50.5 0.0 copy-start
  50.6 1.0 %copy-done = f32[2048,128]{1,0:T(8,128)} copy-done((f32[2048,128]{1,0:T(8,128)}, f32[2048,128]{1,0:T(8,128)S(1)}, u32[]{:S(2)}) %copy-start) | copy-done | bytes 1048600
  51.5 0.0 copy-start.2
  51.5 0.9 %copy-done.2 = f32[1280,128]{1,0:T(8,128)} copy-done((f32[1280,128]{1,0:T(8,128)}, f32[1280,128]{1,0:T(8,128)S(1)}, u32[]{:S(2)}) %copy-start.2) | copy-done | bytes 655384
  52.4 2.6 %shard_map.137 = (f32[8,256]{1,0:T(8,128)}, f32[256,256]{1,0:T(8,128)}, f32[256,768]{1,0:T(8,128)}, f32[3,256]{1,0:T(4,128)}, f32[256,256]{1,0:T(8,128)}, /*index=5*/f32[256,256]{1,0:T(8,128)}) custom-call(f32[2048,128]{1,0:T(8,128)} %copy-done, f32[1280,128]{1,0:T(8,128)} %copy-done.2), custom_call_target="tpu_custom_call" | custom-call | tf_op jit(solution)/shard_map/pallas_call | solution.py:459
Async XLA Ops:
  0.6 1.1 %copy-start.1 = (f32[256,768]{1,0:T(8,128)S(1)}, f32[256,768]{1,0:T(8,128)}, u32[]{:S(2)}) copy-start(f32[256,768]{1,0:T(8,128)} %refs_5_.1) | copy-start | bytes 2359300
  1.8 0.9 %copy-start.3 = (f32[256,256]{1,0:T(8,128)S(1)}, f32[256,256]{1,0:T(8,128)}, u32[]{:S(2)}) copy-start(f32[256,256]{1,0:T(8,128)} %refs_4_.1) | copy-start | bytes 786436
  2.7 0.9 %copy-start.4 = (f32[256,256]{1,0:T(8,128)S(1)}, f32[256,256]{1,0:T(8,128)}, u32[]{:S(2)}) copy-start(f32[256,256]{1,0:T(8,128)} %refs_7_.1) | copy-start | bytes 786436
  3.7 0.9 %copy-start.5 = (f32[256,256]{1,0:T(8,128)S(1)}, f32[256,256]{1,0:T(8,128)}, u32[]{:S(2)}) copy-start(f32[256,256]{1,0:T(8,128)} %refs_8_.1) | copy-start | bytes 786436
  4.6 0.8 %copy-start.6 = (f32[3,2048]{1,0:T(4,128)S(1)}, f32[3,2048]{1,0:T(4,128)}, u32[]{:S(2)}) copy-start(f32[3,2048]{1,0:T(4,128)} %refs_1_.1) | copy-start | bytes 73732
  5.4 0.7 %copy-start.7 = (f32[8,256]{1,0:T(8,128)S(1)}, f32[8,256]{1,0:T(8,128)}, u32[]{:S(2)}) copy-start(f32[8,256]{1,0:T(8,128)} %refs_3_.1) | copy-start | bytes 24580
  6.1 0.7 %copy-start.8 = (f32[8,128]{1,0:T(8,128)S(1)}, f32[8,128]{1,0:T(8,128)}, u32[]{:S(2)}) copy-start(f32[8,128]{1,0:T(8,128)} %refs_0_.1) | copy-start | bytes 12292
  6.8 0.7 %copy-start.9 = (f32[3,256]{1,0:T(4,128)S(1)}, f32[3,256]{1,0:T(4,128)}, u32[]{:S(2)}) copy-start(f32[3,256]{1,0:T(4,128)} %refs_6_.1) | copy-start | bytes 9220
  50.5 1.0 %copy-start = (f32[2048,128]{1,0:T(8,128)}, f32[2048,128]{1,0:T(8,128)S(1)}, u32[]{:S(2)}) copy-start(f32[2048,128]{1,0:T(8,128)S(1)} %get-tuple-element.8.flat_b) | copy-start | bytes 3145732
  51.5 0.9 %copy-start.2 = (f32[1280,128]{1,0:T(8,128)}, f32[1280,128]{1,0:T(8,128)S(1)}, u32[]{:S(2)}) copy-start(f32[1280,128]{1,0:T(8,128)S(1)} %get-tuple-element.9.flat_t) | copy-start | bytes 1966084
